TPU v7x, 256 devices: a whole 4x4x8 slice. The times are simulated.
256 devices in a mesh: seq: 8 (over y, x_hi), head: 32 (over x_lo, z, core).
Axes of the slice: x: 4 (x_hi: 2, x_lo: 2; x = x_hi * 2 + x_lo), y: 4, z: 8, core: 2. Of those that a mesh axis runs over, the one named last changes fastest.
Arguments:
- tokens: bfloat16 [4, 2048, 3072], P(None, ('seq', 'head')), may hold values from -6 to 6
- qkv_weight: bfloat16 [2, 32, 192, 3072], P(None, 'head'), may hold values from -0.109375 to 0.109375
- rate_weight: bfloat16 [2, 32, 3072], P(None, 'head'), may hold values from -0.109375 to 0.109375
- first_init: float32 [2, 32, 64, 256], P(None, 'head'), may hold values from -0.75 to 0.75
- first_bias: float32 [2, 32, 256], P(None, 'head'), may hold values from -3 to 3
- second_init: float32 [2, 32, 256, 64], P(None, 'head'), may hold values from -0.375 to 0.375
- second_bias: float32 [2, 32, 64], P(None, 'head'), may hold values from -3 to 3
- norm_gain: float32 [2, 32, 64], P(None, 'head'), may hold values from 0.25 to 1.75
- norm_bias: float32 [2, 32, 64], P(None, 'head'), may hold values from -3 to 3
- out_weight: bfloat16 [2, 2048, 3072], P(None, 'head'), may hold values from -0.125 to 0.125
Outputs:
- result: bfloat16 [4, 2048, 3072], P(None, ('seq', 'head'))
All inputs are finite; a program needn't handle non-finite values.
Results may differ from a plain program's by a relative error of at most 0.008.
Values may be sent and summed in bfloat16 or wider, within the bound.
A program may use at most 128 MiB of HBM per device.

v0:
```python
import jax
import jax.numpy as jnp
from jax import lax
from jax.sharding import PartitionSpec as P

HEAD_SIZE = 64
MINI = 64


eps = 1e-06


def passed_along(block, axis, distance):
    devices = range(lax.axis_size(axis))
    route = [(i - distance, i) for i in devices if i - distance in devices]
    return lax.ppermute(block, axis, route)


def gelu_pair(z):
    coef = 0.7978845608028654
    inner = coef * (z + 0.044715 * z * z * z)
    tanh_val = jnp.tanh(inner)
    value = 0.5 * z * (1.0 + tanh_val)
    slope = 0.5 * (1.0 + tanh_val) + 0.5 * z * (1.0 - tanh_val * tanh_val) * coef * (
        1.0 + 3.0 * 0.044715 * z * z
    )
    return (value, slope)


def norm_parts(z, gain, shift):
    center = z - jnp.mean(z, axis=-1, keepdims=True)
    inverse = lax.rsqrt(jnp.mean(center * center, axis=-1, keepdims=True) + eps)
    normed = center * inverse
    return (normed, inverse, gain * normed + shift)


def mini_step(state, batch, gain, shift):
    w_first, b_first, w_second, b_second = state
    queries, keys, values, rates = batch
    high = lax.Precision.HIGHEST

    def matmul(left, right):
        return jnp.dot(left, right, precision=high)

    z_one = matmul(keys, w_first) + b_first
    act_one, slope = gelu_pair(z_one)
    z_two = matmul(act_one, w_second) + b_second
    normed, inverse, recon = norm_parts(z_two, gain, shift)
    grad_hat = (recon - (values - keys)) * gain
    width = z_two.shape[-1]
    grad_two = (
        inverse
        / width
        * (
            width * grad_hat
            - jnp.sum(grad_hat, axis=-1, keepdims=True)
            - normed * jnp.sum(grad_hat * normed, axis=-1, keepdims=True)
        )
    )
    grad_one = matmul(grad_two, w_second.T) * slope
    count = queries.shape[0]
    lower = (
        lax.broadcasted_iota(jnp.int32, (count, count), 0)
        >= lax.broadcasted_iota(jnp.int32, (count, count), 1)
    ).astype(jnp.float32)
    weights = lower * rates[None, :]
    z_bar = (
        matmul(queries, w_first)
        + b_first
        - matmul(weights * matmul(queries, keys.T), grad_one)
        - matmul(weights, grad_one)
    )
    act_bar, unused = gelu_pair(z_bar)
    z_bar_two = (
        matmul(act_bar, w_second)
        + b_second
        - matmul(weights * matmul(act_bar, act_one.T), grad_two)
        - matmul(weights, grad_two)
    )
    unused_a, unused_b, final = norm_parts(z_bar_two, gain, shift)
    output = queries + final
    new_first = w_first - matmul((keys * rates[:, None]).T, grad_one)
    new_bfirst = b_first - matmul(rates[None, :], grad_one)[0]
    new_second = w_second - matmul((act_one * rates[:, None]).T, grad_two)
    new_bsecond = b_second - matmul(rates[None, :], grad_two)[0]
    return ((new_first, new_bfirst, new_second, new_bsecond), output)


def ttt_run(state, queries, keys, values, rates, gain, shift):
    length, size = queries.shape
    blocks = length // MINI
    batches = (
        queries.reshape(blocks, MINI, size),
        keys.reshape(blocks, MINI, size),
        values.reshape(blocks, MINI, size),
        rates.reshape(blocks, MINI),
    )
    final, outputs = lax.scan(
        lambda carry, batch: mini_step(carry, batch, gain, shift), state, batches
    )
    return (final, outputs.reshape(length, size))


def pack_state(state):
    return jnp.concatenate([state[0].reshape(-1), state[1], state[2].reshape(-1), state[3]])


def unpack_state(flat, size, hidden):
    first_end = size * hidden
    second_end = first_end + hidden
    third_end = second_end + hidden * size
    return (
        flat[:first_end].reshape(size, hidden),
        flat[first_end:second_end],
        flat[second_end:third_end].reshape(hidden, size),
        flat[third_end:],
    )


def run_chain(init_flat, queries, keys, values, rates, gain, shift, hidden, forward):
    count = lax.axis_size("seq")
    index = lax.axis_index("seq")
    place = index if forward else count - 1 - index
    seqs, length, size = queries.shape
    outputs = jnp.zeros((seqs, length, size), jnp.float32)

    def process(state_in, seq_id, outs):
        pick = lambda arr: lax.dynamic_index_in_dim(arr, seq_id, 0, keepdims=False)
        final, result = ttt_run(
            unpack_state(state_in, size, hidden),
            pick(queries),
            pick(keys),
            pick(values),
            pick(rates),
            gain,
            shift,
        )
        return (pack_state(final), lax.dynamic_update_index_in_dim(outs, result, seq_id, 0))

    def seq_body(seq_id, carry):

        def section(step, inner):
            state, outs = inner
            if forward:
                incoming = passed_along(state, "seq", 1)
            else:
                incoming = passed_along(state, "seq", -1)
            state_in = jnp.where(place == 0, init_flat, incoming)
            return lax.cond(
                place == step, lambda: process(state_in, seq_id, outs), lambda: (state, outs)
            )

        return lax.fori_loop(0, count, section, carry)

    state, outputs = lax.fori_loop(0, seqs, seq_body, (init_flat, outputs))
    return outputs


def heads_out(
    full_rows,
    layer,
    forward,
    qkv_weight,
    rate_weight,
    first_init,
    first_bias,
    second_init,
    second_bias,
    norm_gain,
    norm_bias,
):
    mixed = jnp.einsum(
        "bld,ed->ble", full_rows, qkv_weight[layer][0], preferred_element_type=jnp.float32
    )
    logits = jnp.einsum(
        "bld,d->bl", full_rows, rate_weight[layer][0], preferred_element_type=jnp.float32
    )
    rates = jax.nn.sigmoid(logits) / HEAD_SIZE
    size = mixed.shape[-1] // 3
    queries = mixed[..., :size]
    keys = mixed[..., size : 2 * size]
    values = mixed[..., 2 * size :]
    if not forward:
        queries = jnp.flip(queries, 1)
        keys = jnp.flip(keys, 1)
        values = jnp.flip(values, 1)
        rates = jnp.flip(rates, 1)
    hidden = first_init.shape[-1]
    init_flat = pack_state(
        (first_init[layer][0], first_bias[layer][0], second_init[layer][0], second_bias[layer][0])
    )
    outputs = run_chain(
        init_flat,
        queries,
        keys,
        values,
        rates,
        norm_gain[layer][0],
        norm_bias[layer][0],
        hidden,
        forward,
    )
    if not forward:
        outputs = jnp.flip(outputs, 1)
    return outputs.astype(jnp.bfloat16)


def body(
    tokens,
    qkv_weight,
    rate_weight,
    first_init,
    first_bias,
    second_init,
    second_bias,
    norm_gain,
    norm_bias,
    out_weight,
):
    full_rows = lax.all_gather(tokens, "head", axis=1, tiled=True)
    first_out = heads_out(
        full_rows,
        0,
        True,
        qkv_weight,
        rate_weight,
        first_init,
        first_bias,
        second_init,
        second_bias,
        norm_gain,
        norm_bias,
    )
    first_terms = jnp.einsum(
        "blh,hd->bld", first_out, out_weight[0], preferred_element_type=jnp.float32
    )
    summed = lax.psum(first_terms, "head")
    middle_full = (full_rows.astype(jnp.float32) + summed).astype(jnp.bfloat16)
    rows_here = tokens.shape[1]
    middle_local = lax.dynamic_slice_in_dim(
        middle_full, lax.axis_index("head") * rows_here, rows_here, 1
    )
    second_out = heads_out(
        middle_full,
        1,
        False,
        qkv_weight,
        rate_weight,
        first_init,
        first_bias,
        second_init,
        second_bias,
        norm_gain,
        norm_bias,
    )
    second_terms = jnp.einsum(
        "blh,hd->bld", second_out, out_weight[1], preferred_element_type=jnp.float32
    )
    second_shares = lax.psum_scatter(second_terms, "head", scatter_dimension=1, tiled=True)
    return (middle_local.astype(jnp.float32) + second_shares).astype(jnp.bfloat16)


def solution(mesh):
    placed = (
        P(None, ("seq", "head"), None),
        P(None, "head", None, None),
        P(None, "head", None),
        P(None, "head", None, None),
        P(None, "head", None),
        P(None, "head", None, None),
        P(None, "head", None),
        P(None, "head", None),
        P(None, "head", None),
        P(None, "head", None),
    )
    return jax.shard_map(
        body, mesh=mesh, in_specs=placed, out_specs=P(None, ("seq", "head"), None), check_vma=False
    )
```

profile of v0, /device:TPU:8, one launch (start us, length us, event | category | flops | bytes accessed | tf_op | source)
XLA Modules:
  0.0 1733.4 jit_solution(6032861056746168881)
XLA Ops:
  14.4 68.0 %all-gather.2.cloned.1.call-done = bf16[4,256,3072]{2,1,0:T(8,128)(2,1)} async-done(((bf16[4,8,3072]{2,1,0:T(8,128)(2,1)}), bf16[4,256,3072]{2,1,0:T(8,128)(2,1)}) %all-gather.2.cloned.1.call-update) | async-done | bytes 6291472 | tf_op jit(solution)/shard_map/all_gather | solution.py:220
  89.7 560.4 %while.127 = (s32[]{:T(128)}, f32[33088]{0:T(1024)S(1)}, bf16[4,256,64]{2,1,0:T(8,128)(2,1)S(1)}, s32[]{:T(128)}, pred[]{:T(512)}, /*index=5*/f32[33088]{0:T(102...) while((s32[]{:T(128)}, f32[33088]{0:T(1024)S(1)}, ...), condition=%wide.region_13.14_spmd, body=%wide.region_0.13_spmd.sunk | while | flops 136767104 | bytes 5566840 | solution.py:155
  89.7 141.6 %while.130 = (s32[]{:T(128)}, f32[33088]{0:T(1024)S(1)}, bf16[4,256,64]{2,1,0:T(8,128)(2,1)S(1)}, s32[]{:T(128)}, pred[]{:T(512)}, /*index=5*/f32[33088]{0:T(102...) while((s32[]{:T(128)}, f32[33088]{0:T(1024)S(1)}, ...), condition=%wide.region_12.12_spmd, body=%wide.region_1.11_spmd.sunk | while | flops 136767104 | bytes 5566579 | solution.py:153
  112.3 32.4 %collective-permute-done.1 = f32[33088]{0:T(1024)S(1)} collective-permute-done((f32[33088]{0:T(1024)S(1)}, f32[33088]{0:T(1024)S(1)}, u32[]{:S(2)}, u32[]{:S(2)}) %collective-permute-start.1) | collective-permute-done | bytes 132384 | tf_op jit(solution)/shard_map/while/body/eval_jaxpr/while/body/eval_jaxpr/ppermute | solution.py:16
  231.3 139.8 %while.130 = (s32[]{:T(128)}, f32[33088]{0:T(1024)S(1)}, bf16[4,256,64]{2,1,0:T(8,128)(2,1)S(1)}, s32[]{:T(128)}, pred[]{:T(512)}, /*index=5*/f32[33088]{0:T(102...) while((s32[]{:T(128)}, f32[33088]{0:T(1024)S(1)}, ...), condition=%wide.region_12.12_spmd, body=%wide.region_1.11_spmd.sunk | while | flops 136767104 | bytes 5566579 | solution.py:153
  261.7 20.2 %collective-permute-start.1 = (f32[33088]{0:T(1024)S(1)}, f32[33088]{0:T(1024)S(1)}, u32[]{:S(2)}, u32[]{:S(2)}) collective-permute-start(f32[33088]{0:T(1024)S(1)} %get-tuple-element.2290), channel_id=1, source_target_pairs={{0,32},{32,64},{64,96},{96,128},{128,160},{160,192},{192,224},{1,3... | collective-permute-start | bytes 397064 | tf_op jit(solution)/shard_map/while/body/eval_jaxpr/while/body/eval_jaxpr/ppermute | solution.py:16
  371.1 138.5 %while.130 = (s32[]{:T(128)}, f32[33088]{0:T(1024)S(1)}, bf16[4,256,64]{2,1,0:T(8,128)(2,1)S(1)}, s32[]{:T(128)}, pred[]{:T(512)}, /*index=5*/f32[33088]{0:T(102...) while((s32[]{:T(128)}, f32[33088]{0:T(1024)S(1)}, ...), condition=%wide.region_12.12_spmd, body=%wide.region_1.11_spmd.sunk | while | flops 136767104 | bytes 5566579 | solution.py:153
  509.6 140.4 %while.130 = (s32[]{:T(128)}, f32[33088]{0:T(1024)S(1)}, bf16[4,256,64]{2,1,0:T(8,128)(2,1)S(1)}, s32[]{:T(128)}, pred[]{:T(512)}, /*index=5*/f32[33088]{0:T(102...) while((s32[]{:T(128)}, f32[33088]{0:T(1024)S(1)}, ...), condition=%wide.region_12.12_spmd, body=%wide.region_1.11_spmd.sunk | while | flops 136767104 | bytes 5566579 | solution.py:153
  587.0 19.3 %collective-permute-start.1 = (f32[33088]{0:T(1024)S(1)}, f32[33088]{0:T(1024)S(1)}, u32[]{:S(2)}, u32[]{:S(2)}) collective-permute-start(f32[33088]{0:T(1024)S(1)} %get-tuple-element.2290), channel_id=1, source_target_pairs={{0,32},{32,64},{64,96},{96,128},{128,160},{160,192},{192,224},{1,3... | collective-permute-start | bytes 397064 | tf_op jit(solution)/shard_map/while/body/eval_jaxpr/while/body/eval_jaxpr/ppermute | solution.py:16
  618.4 19.7 %collective-permute-start.1 = (f32[33088]{0:T(1024)S(1)}, f32[33088]{0:T(1024)S(1)}, u32[]{:S(2)}, u32[]{:S(2)}) collective-permute-start(f32[33088]{0:T(1024)S(1)} %get-tuple-element.2290), channel_id=1, source_target_pairs={{0,32},{32,64},{64,96},{96,128},{128,160},{160,192},{192,224},{1,3... | collective-permute-start | bytes 397064 | tf_op jit(solution)/shard_map/while/body/eval_jaxpr/while/body/eval_jaxpr/ppermute | solution.py:16
  657.4 304.6 %all-reduce.2.cloned.1.call-done = f32[4,256,3072]{2,1,0:T(8,128)} async-done(((f32[4,256,3072]{2,1,0:T(8,128)}), f32[4,256,3072]{2,1,0:T(8,128)}) %all-reduce.2.cloned.1.call-update) | async-done | bytes 12582928 | tf_op jit(solution)/shard_map/psum | solution.py:237
  981.7 590.7 %while.129 = (s32[]{:T(128)}, f32[33088]{0:T(1024)S(1)}, bf16[4,256,64]{2,1,0:T(8,128)(2,1)S(1)}, s32[]{:T(128)}, pred[]{:T(512)}, /*index=5*/f32[33088]{0:T(102...) while((s32[]{:T(128)}, f32[33088]{0:T(1024)S(1)}, ...), condition=%wide.region_28.29_spmd, body=%wide.region_15.28_spmd.sunk | while | flops 136767104 | bytes 5566856 | solution.py:155
  981.7 174.0 %while.131 = (s32[]{:T(128)}, f32[33088]{0:T(1024)S(1)}, bf16[4,256,64]{2,1,0:T(8,128)(2,1)S(1)}, s32[]{:T(128)}, pred[]{:T(512)}, /*index=5*/f32[33088]{0:T(102...) while((s32[]{:T(128)}, f32[33088]{0:T(1024)S(1)}, ...), condition=%wide.region_27.27_spmd, body=%wide.region_16.26_spmd.sunk | while | flops 136767104 | bytes 5566579 | solution.py:153
  1032.9 73.9 %collective-permute-done = f32[33088]{0:T(1024)S(1)} collective-permute-done((f32[33088]{0:T(1024)S(1)}, f32[33088]{0:T(1024)S(1)}, u32[]{:S(2)}, u32[]{:S(2)}) %collective-permute-start) | collective-permute-done | bytes 132384 | tf_op jit(solution)/shard_map/while/body/eval_jaxpr/while/body/eval_jaxpr/ppermute | solution.py:16
  1155.7 138.6 %while.131 = (s32[]{:T(128)}, f32[33088]{0:T(1024)S(1)}, bf16[4,256,64]{2,1,0:T(8,128)(2,1)S(1)}, s32[]{:T(128)}, pred[]{:T(512)}, /*index=5*/f32[33088]{0:T(102...) while((s32[]{:T(128)}, f32[33088]{0:T(1024)S(1)}, ...), condition=%wide.region_27.27_spmd, body=%wide.region_16.26_spmd.sunk | while | flops 136767104 | bytes 5566579 | solution.py:153
  1218.9 27.8 %collective-permute-done = f32[33088]{0:T(1024)S(1)} collective-permute-done((f32[33088]{0:T(1024)S(1)}, f32[33088]{0:T(1024)S(1)}, u32[]{:S(2)}, u32[]{:S(2)}) %collective-permute-start) | collective-permute-done | bytes 132384 | tf_op jit(solution)/shard_map/while/body/eval_jaxpr/while/body/eval_jaxpr/ppermute | solution.py:16
  1272.0 19.7 %collective-permute-start = (f32[33088]{0:T(1024)S(1)}, f32[33088]{0:T(1024)S(1)}, u32[]{:S(2)}, u32[]{:S(2)}) collective-permute-start(f32[33088]{0:T(1024)S(1)} %get-tuple-element.2205), channel_id=1, source_target_pairs={{32,0},{64,32},{96,64},{128,96},{160,128},{192,160},{224,192},{33,... | collective-permute-start | bytes 397064 | tf_op jit(solution)/shard_map/while/body/eval_jaxpr/while/body/eval_jaxpr/ppermute | solution.py:16
  1294.3 137.9 %while.131 = (s32[]{:T(128)}, f32[33088]{0:T(1024)S(1)}, bf16[4,256,64]{2,1,0:T(8,128)(2,1)S(1)}, s32[]{:T(128)}, pred[]{:T(512)}, /*index=5*/f32[33088]{0:T(102...) while((s32[]{:T(128)}, f32[33088]{0:T(1024)S(1)}, ...), condition=%wide.region_27.27_spmd, body=%wide.region_16.26_spmd.sunk | while | flops 136767104 | bytes 5566579 | solution.py:153
  1358.7 25.8 %collective-permute-done = f32[33088]{0:T(1024)S(1)} collective-permute-done((f32[33088]{0:T(1024)S(1)}, f32[33088]{0:T(1024)S(1)}, u32[]{:S(2)}, u32[]{:S(2)}) %collective-permute-start) | collective-permute-done | bytes 132384 | tf_op jit(solution)/shard_map/while/body/eval_jaxpr/while/body/eval_jaxpr/ppermute | solution.py:16
  1409.9 19.7 %collective-permute-start = (f32[33088]{0:T(1024)S(1)}, f32[33088]{0:T(1024)S(1)}, u32[]{:S(2)}, u32[]{:S(2)}) collective-permute-start(f32[33088]{0:T(1024)S(1)} %get-tuple-element.2205), channel_id=1, source_target_pairs={{32,0},{64,32},{96,64},{128,96},{160,128},{192,160},{224,192},{33,... | collective-permute-start | bytes 397064 | tf_op jit(solution)/shard_map/while/body/eval_jaxpr/while/body/eval_jaxpr/ppermute | solution.py:16
  1432.1 140.3 %while.131 = (s32[]{:T(128)}, f32[33088]{0:T(1024)S(1)}, bf16[4,256,64]{2,1,0:T(8,128)(2,1)S(1)}, s32[]{:T(128)}, pred[]{:T(512)}, /*index=5*/f32[33088]{0:T(102...) while((s32[]{:T(128)}, f32[33088]{0:T(1024)S(1)}, ...), condition=%wide.region_27.27_spmd, body=%wide.region_16.26_spmd.sunk | while | flops 136767104 | bytes 5566579 | solution.py:153
  1498.4 26.4 %collective-permute-done = f32[33088]{0:T(1024)S(1)} collective-permute-done((f32[33088]{0:T(1024)S(1)}, f32[33088]{0:T(1024)S(1)}, u32[]{:S(2)}, u32[]{:S(2)}) %collective-permute-start) | collective-permute-done | bytes 132384 | tf_op jit(solution)/shard_map/while/body/eval_jaxpr/while/body/eval_jaxpr/ppermute | solution.py:16
  1550.1 19.7 %collective-permute-start = (f32[33088]{0:T(1024)S(1)}, f32[33088]{0:T(1024)S(1)}, u32[]{:S(2)}, u32[]{:S(2)}) collective-permute-start(f32[33088]{0:T(1024)S(1)} %get-tuple-element.2205), channel_id=1, source_target_pairs={{32,0},{64,32},{96,64},{128,96},{160,128},{192,160},{224,192},{33,... | collective-permute-start | bytes 397064 | tf_op jit(solution)/shard_map/while/body/eval_jaxpr/while/body/eval_jaxpr/ppermute | solution.py:16
  1579.2 145.9 %reduce-scatter.2.cloned.1.call-done = f32[4,8,3072]{2,1,0:T(8,128)} async-done(((f32[4,256,3072]{2,1,0:T(8,128)}), f32[4,8,3072]{2,1,0:T(8,128)}) %reduce-scatter.2.cloned.1.call-update) | async-done | bytes 393232 | tf_op jit(solution)/shard_map/reduce_scatter | solution.py:259
  (1375 shorter events, 1151.8 us)
Async XLA Ops:
  6.5 75.8 %all-gather.2.cloned.1.call-start = ((), (), s32[]{:S(2)}) async-start(), calls=%async_computation.1 | async-start | bytes 6488064 | tf_op jit(solution)/shard_map/all_gather | solution.py:220
  7.3 954.8 %all-reduce.2.cloned.1.call-start = ((), (), s32[]{:S(2)}) async-start(), calls=%async_computation.2 | async-start | bytes 25165824 | tf_op jit(solution)/shard_map/psum | solution.py:237
  109.2 35.5 %collective-permute-start.1 = (f32[33088]{0:T(1024)S(1)}, f32[33088]{0:T(1024)S(1)}, u32[]{:S(2)}, u32[]{:S(2)}) collective-permute-start(f32[33088]{0:T(1024)S(1)} %get-tuple-element.2290), channel_id=1, source_target_pairs={{0,32},{32,64},{64,96},{96,128},{128,160},{160,192},{192,224},{1,3... | collective-permute-start | bytes 397064 | tf_op jit(solution)/shard_map/while/body/eval_jaxpr/while/body/eval_jaxpr/ppermute | solution.py:16
  200.6 21.4 %collective-permute-start.1 = (f32[33088]{0:T(1024)S(1)}, f32[33088]{0:T(1024)S(1)}, u32[]{:S(2)}, u32[]{:S(2)}) collective-permute-start(f32[33088]{0:T(1024)S(1)} %get-tuple-element.2290), channel_id=1, source_target_pairs={{0,32},{32,64},{64,96},{96,128},{128,160},{160,192},{192,224},{1,3... | collective-permute-start | bytes 397064 | tf_op jit(solution)/shard_map/while/body/eval_jaxpr/while/body/eval_jaxpr/ppermute | solution.py:16
  231.3 21.1 %collective-permute-start.1 = (f32[33088]{0:T(1024)S(1)}, f32[33088]{0:T(1024)S(1)}, u32[]{:S(2)}, u32[]{:S(2)}) collective-permute-start(f32[33088]{0:T(1024)S(1)} %get-tuple-element.2290), channel_id=1, source_target_pairs={{0,32},{32,64},{64,96},{96,128},{128,160},{160,192},{192,224},{1,3... | collective-permute-start | bytes 397064 | tf_op jit(solution)/shard_map/while/body/eval_jaxpr/while/body/eval_jaxpr/ppermute | solution.py:16
  261.7 22.7 %collective-permute-start.1 = (f32[33088]{0:T(1024)S(1)}, f32[33088]{0:T(1024)S(1)}, u32[]{:S(2)}, u32[]{:S(2)}) collective-permute-start(f32[33088]{0:T(1024)S(1)} %get-tuple-element.2290), channel_id=1, source_target_pairs={{0,32},{32,64},{64,96},{96,128},{128,160},{160,192},{192,224},{1,3... | collective-permute-start | bytes 397064 | tf_op jit(solution)/shard_map/while/body/eval_jaxpr/while/body/eval_jaxpr/ppermute | solution.py:16
  340.4 21.4 %collective-permute-start.1 = (f32[33088]{0:T(1024)S(1)}, f32[33088]{0:T(1024)S(1)}, u32[]{:S(2)}, u32[]{:S(2)}) collective-permute-start(f32[33088]{0:T(1024)S(1)} %get-tuple-element.2290), channel_id=1, source_target_pairs={{0,32},{32,64},{64,96},{96,128},{128,160},{160,192},{192,224},{1,3... | collective-permute-start | bytes 397064 | tf_op jit(solution)/shard_map/while/body/eval_jaxpr/while/body/eval_jaxpr/ppermute | solution.py:16
  400.9 21.4 %collective-permute-start.1 = (f32[33088]{0:T(1024)S(1)}, f32[33088]{0:T(1024)S(1)}, u32[]{:S(2)}, u32[]{:S(2)}) collective-permute-start(f32[33088]{0:T(1024)S(1)} %get-tuple-element.2290), channel_id=1, source_target_pairs={{0,32},{32,64},{64,96},{96,128},{128,160},{160,192},{192,224},{1,3... | collective-permute-start | bytes 397064 | tf_op jit(solution)/shard_map/while/body/eval_jaxpr/while/body/eval_jaxpr/ppermute | solution.py:16
  448.5 21.1 %collective-permute-start.1 = (f32[33088]{0:T(1024)S(1)}, f32[33088]{0:T(1024)S(1)}, u32[]{:S(2)}, u32[]{:S(2)}) collective-permute-start(f32[33088]{0:T(1024)S(1)} %get-tuple-element.2290), channel_id=1, source_target_pairs={{0,32},{32,64},{64,96},{96,128},{128,160},{160,192},{192,224},{1,3... | collective-permute-start | bytes 397064 | tf_op jit(solution)/shard_map/while/body/eval_jaxpr/while/body/eval_jaxpr/ppermute | solution.py:16
  479.1 21.2 %collective-permute-start.1 = (f32[33088]{0:T(1024)S(1)}, f32[33088]{0:T(1024)S(1)}, u32[]{:S(2)}, u32[]{:S(2)}) collective-permute-start(f32[33088]{0:T(1024)S(1)} %get-tuple-element.2290), channel_id=1, source_target_pairs={{0,32},{32,64},{64,96},{96,128},{128,160},{160,192},{192,224},{1,3... | collective-permute-start | bytes 397064 | tf_op jit(solution)/shard_map/while/body/eval_jaxpr/while/body/eval_jaxpr/ppermute | solution.py:16
  539.4 21.4 %collective-permute-start.1 = (f32[33088]{0:T(1024)S(1)}, f32[33088]{0:T(1024)S(1)}, u32[]{:S(2)}, u32[]{:S(2)}) collective-permute-start(f32[33088]{0:T(1024)S(1)} %get-tuple-element.2290), channel_id=1, source_target_pairs={{0,32},{32,64},{64,96},{96,128},{128,160},{160,192},{192,224},{1,3... | collective-permute-start | bytes 397064 | tf_op jit(solution)/shard_map/while/body/eval_jaxpr/while/body/eval_jaxpr/ppermute | solution.py:16
  587.0 21.8 %collective-permute-start.1 = (f32[33088]{0:T(1024)S(1)}, f32[33088]{0:T(1024)S(1)}, u32[]{:S(2)}, u32[]{:S(2)}) collective-permute-start(f32[33088]{0:T(1024)S(1)} %get-tuple-element.2290), channel_id=1, source_target_pairs={{0,32},{32,64},{64,96},{96,128},{128,160},{160,192},{192,224},{1,3... | collective-permute-start | bytes 397064 | tf_op jit(solution)/shard_map/while/body/eval_jaxpr/while/body/eval_jaxpr/ppermute | solution.py:16
  618.4 22.3 %collective-permute-start.1 = (f32[33088]{0:T(1024)S(1)}, f32[33088]{0:T(1024)S(1)}, u32[]{:S(2)}, u32[]{:S(2)}) collective-permute-start(f32[33088]{0:T(1024)S(1)} %get-tuple-element.2290), channel_id=1, source_target_pairs={{0,32},{32,64},{64,96},{96,128},{128,160},{160,192},{192,224},{1,3... | collective-permute-start | bytes 397064 | tf_op jit(solution)/shard_map/while/body/eval_jaxpr/while/body/eval_jaxpr/ppermute | solution.py:16
  656.3 1068.7 %reduce-scatter.2.cloned.1.call-start = ((), (), s32[]{:S(2)}) async-start(), calls=%async_computation.3 | async-start | bytes 12976128 | tf_op jit(solution)/shard_map/reduce_scatter | solution.py:259
  1026.6 80.2 %collective-permute-start = (f32[33088]{0:T(1024)S(1)}, f32[33088]{0:T(1024)S(1)}, u32[]{:S(2)}, u32[]{:S(2)}) collective-permute-start(f32[33088]{0:T(1024)S(1)} %get-tuple-element.2205), channel_id=1, source_target_pairs={{32,0},{64,32},{96,64},{128,96},{160,128},{192,160},{224,192},{33,... | collective-permute-start | bytes 397064 | tf_op jit(solution)/shard_map/while/body/eval_jaxpr/while/body/eval_jaxpr/ppermute | solution.py:16
  1133.4 22.2 %collective-permute-start = (f32[33088]{0:T(1024)S(1)}, f32[33088]{0:T(1024)S(1)}, u32[]{:S(2)}, u32[]{:S(2)}) collective-permute-start(f32[33088]{0:T(1024)S(1)} %get-tuple-element.2205), channel_id=1, source_target_pairs={{32,0},{64,32},{96,64},{128,96},{160,128},{192,160},{224,192},{33,... | collective-permute-start | bytes 397064 | tf_op jit(solution)/shard_map/while/body/eval_jaxpr/while/body/eval_jaxpr/ppermute | solution.py:16
  1212.1 34.6 %collective-permute-start = (f32[33088]{0:T(1024)S(1)}, f32[33088]{0:T(1024)S(1)}, u32[]{:S(2)}, u32[]{:S(2)}) collective-permute-start(f32[33088]{0:T(1024)S(1)} %get-tuple-element.2205), channel_id=1, source_target_pairs={{32,0},{64,32},{96,64},{128,96},{160,128},{192,160},{224,192},{33,... | collective-permute-start | bytes 397064 | tf_op jit(solution)/shard_map/while/body/eval_jaxpr/while/body/eval_jaxpr/ppermute | solution.py:16
  1272.0 22.3 %collective-permute-start = (f32[33088]{0:T(1024)S(1)}, f32[33088]{0:T(1024)S(1)}, u32[]{:S(2)}, u32[]{:S(2)}) collective-permute-start(f32[33088]{0:T(1024)S(1)} %get-tuple-element.2205), channel_id=1, source_target_pairs={{32,0},{64,32},{96,64},{128,96},{160,128},{192,160},{224,192},{33,... | collective-permute-start | bytes 397064 | tf_op jit(solution)/shard_map/while/body/eval_jaxpr/while/body/eval_jaxpr/ppermute | solution.py:16
  1303.6 20.5 %collective-permute-start = (f32[33088]{0:T(1024)S(1)}, f32[33088]{0:T(1024)S(1)}, u32[]{:S(2)}, u32[]{:S(2)}) collective-permute-start(f32[33088]{0:T(1024)S(1)} %get-tuple-element.2205), channel_id=1, source_target_pairs={{32,0},{64,32},{96,64},{128,96},{160,128},{192,160},{224,192},{33,... | collective-permute-start | bytes 397064 | tf_op jit(solution)/shard_map/while/body/eval_jaxpr/while/body/eval_jaxpr/ppermute | solution.py:16
  1352.0 32.6 %collective-permute-start = (f32[33088]{0:T(1024)S(1)}, f32[33088]{0:T(1024)S(1)}, u32[]{:S(2)}, u32[]{:S(2)}) collective-permute-start(f32[33088]{0:T(1024)S(1)} %get-tuple-element.2205), channel_id=1, source_target_pairs={{32,0},{64,32},{96,64},{128,96},{160,128},{192,160},{224,192},{33,... | collective-permute-start | bytes 397064 | tf_op jit(solution)/shard_map/while/body/eval_jaxpr/while/body/eval_jaxpr/ppermute | solution.py:16
  1409.9 22.3 %collective-permute-start = (f32[33088]{0:T(1024)S(1)}, f32[33088]{0:T(1024)S(1)}, u32[]{:S(2)}, u32[]{:S(2)}) collective-permute-start(f32[33088]{0:T(1024)S(1)} %get-tuple-element.2205), channel_id=1, source_target_pairs={{32,0},{64,32},{96,64},{128,96},{160,128},{192,160},{224,192},{33,... | collective-permute-start | bytes 397064 | tf_op jit(solution)/shard_map/while/body/eval_jaxpr/while/body/eval_jaxpr/ppermute | solution.py:16
  1441.4 21.7 %collective-permute-start = (f32[33088]{0:T(1024)S(1)}, f32[33088]{0:T(1024)S(1)}, u32[]{:S(2)}, u32[]{:S(2)}) collective-permute-start(f32[33088]{0:T(1024)S(1)} %get-tuple-element.2205), channel_id=1, source_target_pairs={{32,0},{64,32},{96,64},{128,96},{160,128},{192,160},{224,192},{33,... | collective-permute-start | bytes 397064 | tf_op jit(solution)/shard_map/while/body/eval_jaxpr/while/body/eval_jaxpr/ppermute | solution.py:16
  1491.7 33.1 %collective-permute-start = (f32[33088]{0:T(1024)S(1)}, f32[33088]{0:T(1024)S(1)}, u32[]{:S(2)}, u32[]{:S(2)}) collective-permute-start(f32[33088]{0:T(1024)S(1)} %get-tuple-element.2205), channel_id=1, source_target_pairs={{32,0},{64,32},{96,64},{128,96},{160,128},{192,160},{224,192},{33,... | collective-permute-start | bytes 397064 | tf_op jit(solution)/shard_map/while/body/eval_jaxpr/while/body/eval_jaxpr/ppermute | solution.py:16
  1550.1 22.3 %collective-permute-start = (f32[33088]{0:T(1024)S(1)}, f32[33088]{0:T(1024)S(1)}, u32[]{:S(2)}, u32[]{:S(2)}) collective-permute-start(f32[33088]{0:T(1024)S(1)} %get-tuple-element.2205), channel_id=1, source_target_pairs={{32,0},{64,32},{96,64},{128,96},{160,128},{192,160},{224,192},{33,... | collective-permute-start | bytes 397064 | tf_op jit(solution)/shard_map/while/body/eval_jaxpr/while/body/eval_jaxpr/ppermute | solution.py:16
  (55 other events, 1709.4 us)
Sparse Core Ops, SparseCore 0:
  9.2 73.1 all-gather.1
  656.4 305.5 all-reduce.1
  1579.3 145.7 reduce-scatter.1
where the time goes:
time: 1740 us; the launch traced here: 1730 us
  waiting for transfers between devices  908 us (52%)
  starting transfers between devices  626 us (36%)
  matrix products  131 us (8%)
  local copies, waits for them, and re-layouts  24.5 us (1%)
  other arithmetic  23.2 us (1%)
    ppermute x64, starting transfers between devices, passed_along(): return lax.ppermute(block, axis, route)  626 us
    ppermute x64, waiting for transfers between devices, passed_along(): return lax.ppermute(block, axis, route)  389 us
    psum x1, waiting for transfers between devices, body(): summed = lax.psum(first_terms, 'head')  305 us
    reduce_scatter x1, waiting for transfers between devices, body(): lax.psum_scatter(second_terms, 'head', scatter_dimension=1, tiled=True)  146 us
    dot_general x480, matrix products, matmul(): return jnp.dot(left, right, precision=high)  104 us
    all_gather x1, waiting for transfers between devices, body(): full_rows = lax.all_gather(tokens, 'head', axis=1, tiled=True)  68 us
  transfers between devices with their start and end apart: 67, of which 67 were waited for; matrix products, arithmetic and copies ran while one was open for 0% of the time, Pallas kernels for 0%

commit v1 on v0

v1 whole, which is shorter than its diff:
```python
import functools

import jax
import jax.numpy as jnp
from jax import lax
from jax.experimental import pallas as pl
from jax.experimental.pallas import tpu as pltpu
from jax.sharding import PartitionSpec as P

HEAD_SIZE = 64
MINI = 64
EPS = 1e-06
BF = jnp.bfloat16
F32 = jnp.float32


def dot(a, b, dims):
    return lax.dot_general(a, b, (dims, ((), ())), preferred_element_type=F32)


NN = ((1,), (0,))
NT = ((1,), (1,))
TN = ((0,), (0,))


def gelu_pair(z):
    coef = 0.7978845608028654
    zz = z * z
    cube = 0.044715 * coef * zz
    tanh_val = jnp.tanh(z * (coef + cube))
    half = 0.5 + 0.5 * tanh_val
    value = z * half
    slope = half + value * (1.0 - tanh_val) * (coef + 3.0 * cube)
    return value, slope


def split(x):
    high = x.astype(BF)
    return high, (x - high.astype(F32)).astype(BF)


def scan_kernel(
    forward,
    s_ref,
    d_ref,
    r_ref,
    w1_ref,
    b1_ref,
    w2_ref,
    b2_ref,
    g_ref,
    c_ref,
    o_ref,
    w1d,
    b1,
    w2t,
    w2d,
    b2,
    g1h_p,
    g1l_p,
    g2h_p,
    g2l_p,
    th_p,
    tl_p,
    sh_p,
    sl_p,
):
    steps, size, lanes = s_ref.shape
    hidden = w1_ref.shape[1]
    half = lanes // 2
    w1d[...] = jnp.concatenate([w1_ref[...], w1_ref[...]], 0).T
    b1[...] = jnp.broadcast_to(b1_ref[...], (lanes, hidden)).T
    centred = w2_ref[...] - jnp.mean(w2_ref[...], axis=1, keepdims=True)
    w2d[...] = jnp.concatenate([centred, centred], 1)
    w2t[...] = centred.T
    b2[...] = jnp.broadcast_to(b2_ref[...] - jnp.mean(b2_ref[...]), (size, lanes))
    for ref in (g1h_p, g1l_p, g2h_p, g2l_p, th_p, tl_p, sh_p, sl_p):
        ref[...] = jnp.zeros_like(ref)

    row = lax.broadcasted_iota(jnp.int32, (lanes, lanes), 0) - half
    col = lax.broadcasted_iota(jnp.int32, (lanes, lanes), 1)
    seen = (row <= col) if forward else (row >= col)
    first_mask = (seen | (col >= half)).astype(F32)
    second_mask = (~seen & (col < half)).astype(F32)
    low_half = lax.broadcasted_iota(jnp.int32, (hidden, lanes), 1) < half
    gain = jnp.broadcast_to(g_ref[...], (size, lanes))
    shift = jnp.broadcast_to(c_ref[...], (size, lanes))
    gain2 = gain * gain
    ones = jnp.ones((lanes, lanes), BF)
    zeros = jnp.zeros((lanes, lanes), BF)
    blank = jnp.zeros((half, lanes), BF)

    def stacked(doubled):
        high = doubled.astype(BF)
        low = (doubled - high.astype(F32)).astype(BF)
        return jnp.concatenate([jnp.where(low_half, high, low), high], 1)

    def step(j, carry):
        s = s_ref[j]
        sh, sl = split(s)
        shp, slp = sh_p[...], sl_p[...]
        g1h, g1l = g1h_p[...], g1l_p[...]
        g2h, g2l = g2h_p[...], g2l_p[...]
        thp, tlp = th_p[...], tl_p[...]
        g1s = jnp.concatenate([g1h, g1l, g1h], 1)
        g2s = jnp.concatenate([g2h, g2l, g2h], 1)
        w1_old, b1_old = w1d[...], b1[...]
        w2t_new = w2t[...] - dot(g2s, jnp.concatenate([thp, thp, tlp], 1), NT)
        g2dh = jnp.concatenate([g2h, g2h], 0)
        g2dl = jnp.concatenate([g2l, g2l], 0)
        w2d_new = w2d[...] - dot(
            jnp.concatenate([thp, tlp, thp], 1), jnp.concatenate([g2dh, g2dh, g2dl], 1), NT
        )
        b2_new = b2[...] - jnp.sum(g2h.astype(F32) + g2l.astype(F32), axis=1, keepdims=True)
        w2t[...] = w2t_new
        w2d[...] = w2d_new
        b2[...] = b2_new
        sd_high = jnp.concatenate([shp, shp, ones], 0)
        sd_low = jnp.concatenate([slp, slp, zeros], 0)
        change = dot(g1s, jnp.concatenate([sd_high, sd_high, sd_low], 1), NT)
        w1d[...] = w1_old - change[:, :lanes]
        b1[...] = b1_old - change[:, lanes:]
        pair = dot(
            jnp.concatenate([shp, slp, shp], 0), jnp.concatenate([sh, sh, sl], 0), TN
        )
        ph, pl_ = split((pair + 1.0) * first_mask)
        z = (
            dot(stacked(w1_old), jnp.concatenate([sh, sh, sl, blank], 0), NN)
            + b1_old
            - dot(g1s, jnp.concatenate([ph, ph, pl_], 0), NN)
        )
        value, slope = gelu_pair(z)
        th, tl = split(value)
        w2h, w2l = split(w2t_new)
        z2 = (
            dot(
                jnp.concatenate([w2h, w2l, w2h], 1), jnp.concatenate([th, th, tl], 0), NN
            )
            + b2_new
        )
        cross = dot(
            jnp.concatenate([thp, tlp, thp], 0), jnp.concatenate([th, th, tl], 0), TN
        )
        ch, cl = split((cross + 1.0) * second_mask)
        z2o = z2 + dot(g2s, jnp.concatenate([ch, ch, cl], 0), NN)
        d0 = gain * (shift - d_ref[j])
        zz = z2 * z2
        s_zz = jnp.sum(zz, axis=0, keepdims=True)
        s_g = jnp.sum(gain2 * z2, axis=0, keepdims=True)
        s_gzz = jnp.sum(gain2 * zz, axis=0, keepdims=True)
        s_dz = jnp.sum(d0 * z2, axis=0, keepdims=True)
        s_d = jnp.sum(d0, axis=0, keepdims=True)
        inv = lax.rsqrt(s_zz * (1.0 / size) + EPS)
        sum_h = inv * s_g + s_d
        sum_hn = inv * (inv * s_gzz + s_dz)
        n = z2 * inv
        scale = inv * r_ref[j]
        g2h_n, g2l_n = split(scale * (gain2 * n + d0 - (sum_h + n * sum_hn) * (1.0 / size)))
        g1 = (
            dot(stacked(w2d_new), jnp.concatenate([g2h_n, g2h_n, g2l_n, blank], 0), NN) * slope
        )
        g1h_n, g1l_n = split(g1)
        s_oo = jnp.sum(z2o * z2o, axis=0, keepdims=True)
        no = z2o * lax.rsqrt(s_oo * (1.0 / size) + EPS)
        o_ref[j] = (s + gain * no + shift).astype(BF)
        g1h_p[...] = g1h_n
        g1l_p[...] = g1l_n
        g2h_p[...] = g2h_n
        g2l_p[...] = g2l_n
        th_p[...] = th
        tl_p[...] = tl
        sh_p[...] = sh
        sl_p[...] = sl
        return carry

    lax.fori_loop(0, steps, step, 0)


def run_scan(forward, s, d, r, w1, b1, w2, b2, g, c):
    steps, size, lanes = s.shape
    hidden = w1.shape[1]
    vmem = pl.BlockSpec(memory_space=pltpu.VMEM)
    pair = lambda shape: [pltpu.VMEM(shape, BF)] * 2
    return pl.pallas_call(
        functools.partial(scan_kernel, forward),
        out_shape=jax.ShapeDtypeStruct((steps, size, lanes), BF),
        in_specs=[vmem] * 9,
        out_specs=vmem,
        scratch_shapes=[
            pltpu.VMEM((hidden, lanes), F32),
            pltpu.VMEM((hidden, lanes), F32),
            pltpu.VMEM((size, hidden), F32),
            pltpu.VMEM((hidden, lanes), F32),
            pltpu.VMEM((size, lanes), F32),
            *pair((hidden, lanes)),
            *pair((size, lanes)),
            *pair((hidden, lanes)),
            *pair((size, lanes)),
        ],
        compiler_params=pltpu.CompilerParams(vmem_limit_bytes=32 * 2**20),
        cost_estimate=pl.CostEstimate(
            flops=steps * 2 * 3008 * 65536, bytes_accessed=5 * steps * size * lanes * 2, transcendentals=0
        ),
        name="scan_fwd" if forward else "scan_rev",
    )(s, d, r, w1, b1, w2, b2, g, c)


def assemble(chain, forward):
    shards, rows, tokens = chain.shape
    n = shards * tokens // MINI
    blocks = chain.reshape(shards, rows, tokens // MINI, MINI).transpose(0, 2, 1, 3).reshape(n, rows, MINI)
    if not forward:
        blocks = blocks[::-1]
    q = blocks[:, :HEAD_SIZE]
    k = blocks[:, HEAD_SIZE : 2 * HEAD_SIZE]
    v = blocks[:, 2 * HEAD_SIZE : 3 * HEAD_SIZE]
    logit = blocks[:, 3 * HEAD_SIZE : 3 * HEAD_SIZE + 1]
    before = lambda x: jnp.pad(x, ((1, 0), (0, 0), (0, 0)))
    after = lambda x: jnp.pad(x, ((0, 1), (0, 0), (0, 0)))
    s = jnp.concatenate([before(q), after(k)], -1)
    d = jnp.pad(v - k, ((0, 1), (0, 0), (MINI, 0)))
    r = jnp.pad(jax.nn.sigmoid(logit) / HEAD_SIZE, ((0, 1), (0, 0), (MINI, 0)))
    return s, d, r


def chain_heads(mixed, forward, params):
    seqs = mixed.shape[0]
    shards = lax.axis_size("seq")
    copies = shards // seqs
    send = jnp.repeat(mixed, copies, axis=0)
    chain = lax.all_to_all(send, "seq", 0, 0, tiled=True)
    out = run_scan(forward, *assemble(chain, forward), *params)
    o = out[1:, :, :MINI]
    if not forward:
        o = o[::-1]
    n = o.shape[0]
    part = n // shards // copies
    o = o.reshape(shards, copies, part, HEAD_SIZE, MINI)
    mine = lax.dynamic_index_in_dim(o, lax.rem(lax.axis_index("seq"), copies), 1, keepdims=False)
    return mine


def back_to_shards(mine, seqs):
    shards, part, size, mini = mine.shape
    back = lax.all_to_all(mine, "seq", 0, 0, tiled=True)
    return back.reshape(seqs, shards // seqs * part, size, mini)


def body(
    tokens,
    qkv_weight,
    rate_weight,
    first_init,
    first_bias,
    second_init,
    second_bias,
    norm_gain,
    norm_bias,
    out_weight,
):
    seqs, rows_here, width = tokens.shape
    shards = lax.axis_size("seq")
    heads = lax.axis_size("head")
    index = lax.axis_index("seq")
    cut = width // shards

    def weights(layer):
        return jnp.concatenate(
            [qkv_weight[layer, 0], rate_weight[layer], jnp.zeros((7, width), BF)], 0
        )

    def params(layer):
        return (
            first_init[layer, 0],
            first_bias[layer],
            second_init[layer, 0],
            second_bias[layer].T,
            norm_gain[layer].T,
            norm_bias[layer].T,
        )

    def out_slice(layer):
        piece = lax.dynamic_slice_in_dim(out_weight[layer], index * cut, cut, 1)
        return lax.all_gather(piece, "head", axis=0, tiled=True)

    def project(layer, full):
        return jnp.einsum("ed,bld->bel", weights(layer), full, preferred_element_type=F32)

    def own_rows(o):
        split = o.reshape(seqs, -1, HEAD_SIZE, MINI // rows_here, rows_here)
        split = split.transpose(1, 3, 0, 4, 2).reshape(heads, seqs * rows_here, HEAD_SIZE)
        got = lax.all_to_all(split, "head", 0, 0, tiled=True)
        mine = got.transpose(1, 0, 2).reshape(seqs * rows_here, heads * HEAD_SIZE)
        return lax.all_gather(mine, "seq", axis=0, tiled=True)

    def layer_out(layer, local, o, sliced):
        delta = jnp.dot(own_rows(o), sliced, preferred_element_type=F32)
        delta = delta.reshape(shards, seqs * rows_here, cut)
        delta = lax.all_to_all(delta, "seq", 0, 0, tiled=True)
        delta = delta.transpose(1, 0, 2).reshape(seqs, rows_here, width)
        return (local.astype(F32) + delta).astype(BF)

    full = lax.all_gather(tokens, "head", axis=1, tiled=True)
    mixed = project(0, full)
    sliced = out_slice(0), out_slice(1)
    o = back_to_shards(chain_heads(mixed, True, params(0)), seqs)
    middle = layer_out(0, tokens, o, sliced[0])
    full = lax.all_gather(middle, "head", axis=1, tiled=True)
    o = back_to_shards(chain_heads(project(1, full), False, params(1)), seqs)
    return layer_out(1, middle, o, sliced[1])


def solution(mesh):
    placed = (
        P(None, ("seq", "head"), None),
        P(None, "head", None, None),
        P(None, "head", None),
        P(None, "head", None, None),
        P(None, "head", None),
        P(None, "head", None, None),
        P(None, "head", None),
        P(None, "head", None),
        P(None, "head", None),
        P(None, "head", None),
    )
    return jax.shard_map(
        body, mesh=mesh, in_specs=placed, out_specs=P(None, ("seq", "head"), None), check_vma=False
    )
```

time: 1740 us -> 484 us (0.28)
  waiting for transfers between devices: 908 us -> 270 us
  starting transfers between devices: 626 us -> 14.9 us
  matrix products: 131 us -> 14.9 us
  blocking collectives: 0 us -> 77.8 us
  Pallas kernels: 0 us -> 65.7 us
  other arithmetic: 23.2 us -> 3.24 us
    ppermute x64 -> x0, starting transfers between devices: 626 us -> none  [passed_along(): return lax.ppermute(block, axis, route)]
    ppermute x64 -> x0, waiting for transfers between devices: 389 us -> none  [passed_along(): return lax.ppermute(block, axis, route)]
    psum x1 -> x0, waiting for transfers between devices: 305 us -> none  [body(): summed = lax.psum(first_terms, 'head')]
    all_gather x1 -> x6, waiting for transfers between devices: 68 us -> 229 us  [the longest x2 89.1 us: own_rows(): return lax.all_gather(mine, 'seq', axis=0, tiled=True)]
    reduce_scatter x1 -> x0, waiting for transfers between devices: 146 us -> none  [body(): lax.psum_scatter(second_terms, 'head', scatter_dimension=1, tiled=True)]
    dot_general x486 -> x4, matrix products: 131 us -> 14.9 us  [the longest x2 10.1 us: project(): jnp.einsum('ed,bld->bel', weights(layer), full, preferred_element_type=F32)]
    all_to_all x0 -> x6, blocking collectives: none -> 77.8 us  [the longest x2 30.7 us: own_rows(): got = lax.all_to_all(split, 'head', 0, 0, tiled=True)]
    pallas_call x0 -> x2, Pallas kernels: none -> 65.7 us  [run_scan(): pl.pallas_call(functools.partial(scan_kernel, forward), out_shape=jax.Sha...]
  transfers between devices with their start and end apart: 67 -> 8, of which waited for: 67 -> 6; matrix products, arithmetic and copies ran while one was open for 0% -> 4% of each run, Pallas kernels for 0% -> 14%
where the time goes in v1:
time: 484 us; the launch traced here: 483 us
  waiting for transfers between devices  270 us (56%)
  blocking collectives  77.8 us (16%)
  Pallas kernels  65.7 us (14%)
  local copies, waits for them, and re-layouts  21.8 us (5%)
  starting transfers between devices  14.9 us (3%)
  matrix products  14.9 us (3%)
  between operations  13.9 us (3%)
    all_gather x2, waiting for transfers between devices, own_rows(): return lax.all_gather(mine, 'seq', axis=0, tiled=True)  89.1 us
    all_gather x1, waiting for transfers between devices, body(): full = lax.all_gather(tokens, 'head', axis=1, tiled=True)  70.5 us
    all_gather x1, waiting for transfers between devices, body(): full = lax.all_gather(middle, 'head', axis=1, tiled=True)  69.4 us
    pallas_call x2, Pallas kernels, run_scan(): pl.pallas_call(functools.partial(scan_kernel, forward), out_shape=jax.Sha...  65.7 us
    all_to_all x2, waiting for transfers between devices, chain_heads(): chain = lax.all_to_all(send, 'seq', 0, 0, tiled=True)  40.3 us
    all_to_all x2, blocking collectives, own_rows(): got = lax.all_to_all(split, 'head', 0, 0, tiled=True)  30.7 us
    all_to_all x2, blocking collectives, layer_out(): delta = lax.all_to_all(delta, 'seq', 0, 0, tiled=True)  24.8 us
    all_to_all x2, blocking collectives, back_to_shards(): back = lax.all_to_all(mine, 'seq', 0, 0, tiled=True)  22.2 us
  transfers between devices with their start and end apart: 8, of which 6 were waited for; matrix products, arithmetic and copies ran while one was open for 4% of the time, Pallas kernels for 14%

profile of v1, /device:TPU:8, one launch (start us, length us, event | category | flops | bytes accessed | tf_op | source)
XLA Modules:
  0.0 482.5 jit_solution(10077896230361667908)
XLA Ops:
  8.2 1.9 fusion.20
  10.1 1.8 slice_bitcast_fusion
  11.9 70.5 %all-gather.9.cloned.1.call-done = bf16[4,256,3072]{2,1,0:T(8,128)(2,1)} async-done(((bf16[4,8,3072]{2,1,0:T(8,128)(2,1)}), bf16[4,256,3072]{2,1,0:T(8,128)(2,1)}) %all-gather.9.cloned.1.call-update) | async-done | bytes 6291472 | tf_op jit(solution)/shard_map/all_gather | solution.py:303
  82.3 5.0 %convolution_bitcast_fusion.1 = f32[4,200,256]{2,1,0:T(8,128)S(1)} fusion(bf16[4,256,3072]{2,1,0:T(8,128)(2,1)} %all-gather.9.cloned.1.call-done, bf16[1,3072]{1,0:T(2,128)(2,1)S(1)} %get-tuple-element.28, bf16[192,3072]{1,0:T(8,128)(2,1)S(1)} %get-tuple-element.12, bf16[200]{0:T(256)(128)(2,1)S(1)} %pad.53.clone), kind=kOutput, calls=%fused_computation.7 | convolution fusion | flops 1261977600 | bytes 8296848 | tf_op jit(solution)/shard_map/ed,bld->bel/dot_general | solution.py:287
  88.7 7.4 %all-to-all-start = ((f32[8,200,256]{2,1,0:T(8,128)}), f32[8,200,256]{2,1,0:T(8,128)S(1)}, u32[]{:S(2)}, u32[]{:S(2)}) async-start(f32[8,200,256]{2,1,0:T(8,128)} %bitcast.4), calls=%async_computation | async-start | bytes 3276800 | tf_op jit(solution)/shard_map/all_to_all | solution.py:231
  99.3 19.6 %all-to-all-done = f32[8,200,256]{2,1,0:T(8,128)S(1)} async-done(((f32[8,200,256]{2,1,0:T(8,128)}), f32[8,200,256]{2,1,0:T(8,128)S(1)}, u32[]{:S(2)}, u32[]{:S(2)}) %all-to-all-start) | async-done | bytes 1638432 | tf_op jit(solution)/shard_map/all_to_all | solution.py:231
  120.9 32.9 %scan_fwd.1 = bf16[33,64,128]{2,1,0:T(8,128)(2,1)S(1)} custom-call(f32[33,64,128]{2,1,0:T(8,128)S(1)} %select_maximum_fusion.1.s_ref, f32[33,64,128]{2,1,0:T(8,128)S(1)} %pad.30.d_ref, f32[33,1,128]{2,1,0:T(1,128)S(1)} %pad.31.r_ref, f32[64,256]{1,0:T(8,128)S(1)} %get-tuple-element.26.w1_ref, f32[1,256]{1,0:T(1,128)S(1)} %get-tuple-element.30.b1_ref, ...), custom_call_target="tpu_custom_call" | custom-call | flops 13010731008 | bytes 2703360 | tf_op jit(solution)/shard_map/scan_fwd/pallas_call | solution.py:184
  154.4 11.1 %all_to_all.40 = bf16[8,2,4096]{2,1,0:T(2,128)(2,1)S(1)} all-to-all(bf16[8,2,4096]{2,1,0:T(2,128)(2,1)S(1)} %reshape.64), channel_id=1, replica_groups=mesh['seq'=8,'head'=32] {'seq'}, dimensions={0} | all-to-all | bytes 262144 | tf_op jit(solution)/shard_map/all_to_all | solution.py:245
  165.9 15.3 %all_to_all.41 = bf16[32,2,1024]{2,1,0:T(2,128)(2,1)S(1)} all-to-all(bf16[32,2,1024]{2,1,0:T(2,128)(2,1)S(1)} %reshape.66), channel_id=1, replica_groups=mesh['seq'=8,'head'=32] {'head'}, dimensions={0} | all-to-all | bytes 262144 | tf_op jit(solution)/shard_map/all_to_all | solution.py:292
  182.7 44.5 %all-gather.11.cloned.1.call-done = bf16[256,2048]{1,0:T(8,128)(2,1)} async-done(((bf16[32,2048]{1,0:T(8,128)(2,1)}), bf16[256,2048]{1,0:T(8,128)(2,1)}) %all-gather.11.cloned.1.call-update) | async-done | bytes 1048592 | tf_op jit(solution)/shard_map/all_gather | solution.py:294
  227.2 2.4 fusion.2
  229.7 12.4 %all_to_all.42 = f32[8,32,384]{2,1,0:T(8,128)S(1)} all-to-all(f32[8,32,384]{2,1,0:T(8,128)S(1)} %bitcast.93), channel_id=1, replica_groups=mesh['seq'=8,'head'=32] {'seq'}, dimensions={0} | all-to-all | bytes 786432 | tf_op jit(solution)/shard_map/all_to_all | solution.py:299
  243.1 69.4 %all-gather.13.cloned.1.call-done = bf16[4,256,3072]{2,1,0:T(8,128)(2,1)} async-done(((bf16[4,8,3072]{2,1,0:T(8,128)(2,1)}), bf16[4,256,3072]{2,1,0:T(8,128)(2,1)}) %all-gather.13.cloned.1.call-update) | async-done | bytes 6291472 | tf_op jit(solution)/shard_map/all_gather | solution.py:308
  312.6 5.0 %convolution_bitcast_fusion = f32[4,200,256]{2,1,0:T(8,128)S(1)} fusion(bf16[4,256,3072]{2,1,0:T(8,128)(2,1)} %all-gather.13.cloned.1.call-done, bf16[1,3072]{1,0:T(2,128)(2,1)S(1)} %get-tuple-element.27, bf16[192,3072]{1,0:T(8,128)(2,1)S(1)} %get-tuple-element.11, bf16[200]{0:T(256)(128)(2,1)S(1)} %copy-done.6), kind=kOutput, calls=%fused_computation.6 | convolution fusion | flops 1261977600 | bytes 8296848 | tf_op jit(solution)/shard_map/ed,bld->bel/dot_general | solution.py:287
  317.6 1.3 broadcast_in_dim.7
  318.9 7.2 %all-to-all-start.4 = ((f32[8,200,256]{2,1,0:T(8,128)}), f32[8,200,256]{2,1,0:T(8,128)S(1)}, u32[]{:S(2)}, u32[]{:S(2)}) async-start(f32[8,200,256]{2,1,0:T(8,128)} %bitcast.90), calls=%async_computation.4 | async-start | bytes 3276800 | tf_op jit(solution)/shard_map/all_to_all | solution.py:231
  326.2 1.4 constant_dynamic-slice_fusion
  328.2 20.8 %all-to-all-done.4 = f32[8,200,256]{2,1,0:T(8,128)S(1)} async-done(((f32[8,200,256]{2,1,0:T(8,128)}), f32[8,200,256]{2,1,0:T(8,128)S(1)}, u32[]{:S(2)}, u32[]{:S(2)}) %all-to-all-start.4) | async-done | bytes 1638432 | tf_op jit(solution)/shard_map/all_to_all | solution.py:231
  353.5 32.9 %scan_rev.1 = bf16[33,64,128]{2,1,0:T(8,128)(2,1)S(1)} custom-call(f32[33,64,128]{2,1,0:T(8,128)S(1)} %select_maximum_fusion.s_ref, f32[33,64,128]{2,1,0:T(8,128)S(1)} %pad.34.d_ref, f32[33,1,128]{2,1,0:T(1,128)S(1)} %pad.35.r_ref, f32[64,256]{1,0:T(8,128)S(1)} %get-tuple-element.25.w1_ref, f32[1,256]{1,0:T(1,128)S(1)} %get-tuple-element.29.b1_ref, ...), custom_call_target="tpu_custom_call" | custom-call | flops 13010731008 | bytes 2703360 | tf_op jit(solution)/shard_map/scan_rev/pallas_call | solution.py:184
  387.0 11.1 %all_to_all.43 = bf16[8,2,4096]{2,1,0:T(2,128)(2,1)S(1)} all-to-all(bf16[8,2,4096]{2,1,0:T(2,128)(2,1)S(1)} %reshape.68), channel_id=1, replica_groups=mesh['seq'=8,'head'=32] {'seq'}, dimensions={0} | all-to-all | bytes 262144 | tf_op jit(solution)/shard_map/all_to_all | solution.py:245
  398.5 15.4 %all_to_all.44 = bf16[32,2,1024]{2,1,0:T(2,128)(2,1)S(1)} all-to-all(bf16[32,2,1024]{2,1,0:T(2,128)(2,1)S(1)} %reshape.70), channel_id=1, replica_groups=mesh['seq'=8,'head'=32] {'head'}, dimensions={0} | all-to-all | bytes 262144 | tf_op jit(solution)/shard_map/all_to_all | solution.py:292
  415.2 44.6 %all-gather.15.cloned.1.call-done = bf16[256,2048]{1,0:T(8,128)(2,1)} async-done(((bf16[32,2048]{1,0:T(8,128)(2,1)}), bf16[256,2048]{1,0:T(8,128)(2,1)}) %all-gather.15.cloned.1.call-update) | async-done | bytes 1048592 | tf_op jit(solution)/shard_map/all_gather | solution.py:294
  459.8 2.4 fusion
  462.2 12.4 %all_to_all.45 = f32[8,32,384]{2,1,0:T(8,128)S(1)} all-to-all(f32[8,32,384]{2,1,0:T(8,128)S(1)} %bitcast.94), channel_id=1, replica_groups=mesh['seq'=8,'head'=32] {'seq'}, dimensions={0} | all-to-all | bytes 786432 | tf_op jit(solution)/shard_map/all_to_all | solution.py:299
  (95 shorter events, 19.8 us)
Async XLA Ops:
  6.5 75.8 %all-gather.9.cloned.1.call-start = ((), (), s32[]{:S(2)}) async-start(), calls=%async_computation.8 | async-start | bytes 6488064 | tf_op jit(solution)/shard_map/all_gather | solution.py:303
  7.3 75.0 %copy-start.5 = (bf16[200]{0:T(256)(128)(2,1)}, bf16[200]{0:T(256)(128)(2,1)S(1)}, u32[]{:S(2)}) copy-start(bf16[200]{0:T(256)(128)(2,1)S(1)} %pad.53.clone) | copy-start | bytes 1204
  88.7 8.2 %copy-start.2 = (f32[2,1,256,64]{2,3,1,0:T(8,128)S(1)}, f32[2,1,256,64]{2,3,1,0:T(8,128)}, u32[]{:S(2)}) copy-start(f32[2,1,256,64]{2,3,1,0:T(8,128)} %param.15) | copy-start | bytes 393220
  88.7 10.6 %copy-start.4 = (f32[2,1,256]{2,1,0:T(1,128)S(1)}, f32[2,1,256]{2,1,0:T(1,128)}, u32[]{:S(2)}) copy-start(f32[2,1,256]{2,1,0:T(1,128)} %param.14) | copy-start | bytes 6148
  88.7 10.6 %copy-start.3 = (f32[2,1,64,256]{3,2,1,0:T(8,128)S(1)}, f32[2,1,64,256]{3,2,1,0:T(8,128)}, u32[]{:S(2)}) copy-start(f32[2,1,64,256]{3,2,1,0:T(8,128)} %param.13) | copy-start | bytes 393220
  88.7 30.2 %all-to-all-start = ((f32[8,200,256]{2,1,0:T(8,128)}), f32[8,200,256]{2,1,0:T(8,128)S(1)}, u32[]{:S(2)}, u32[]{:S(2)}) async-start(f32[8,200,256]{2,1,0:T(8,128)} %bitcast.4), calls=%async_computation | async-start | bytes 3276800 | tf_op jit(solution)/shard_map/all_to_all | solution.py:231
  96.1 86.6 %all-gather.17.cloned.1.call-start = ((), (), s32[]{:S(2)}) async-start(), calls=%async_computation.12 | async-start | bytes 1622016 | tf_op jit(solution)/shard_map/all_gather | solution.py:284
  96.8 130.4 %all-gather.11.cloned.1.call-start = ((), (), s32[]{:S(2)}) async-start(), calls=%async_computation.9 | async-start | bytes 1179648 | tf_op jit(solution)/shard_map/all_gather | solution.py:294
  182.6 130.0 %all-gather.13.cloned.1.call-start = ((), (), s32[]{:S(2)}) async-start(), calls=%async_computation.10 | async-start | bytes 6488064 | tf_op jit(solution)/shard_map/all_gather | solution.py:308
  229.6 12.7 %copy-start.1 = (bf16[4,8,3072]{2,1,0:T(8,128)(2,1)S(1)}, bf16[4,8,3072]{2,1,0:T(8,128)(2,1)}, u32[]{:S(2)}) copy-start(bf16[4,8,3072]{2,1,0:T(8,128)(2,1)} %param.10) | copy-start | bytes 589828
  229.6 82.9 %copy-start.6 = (bf16[200]{0:T(256)(128)(2,1)S(1)}, bf16[200]{0:T(256)(128)(2,1)}, u32[]{:S(2)}) copy-start(bf16[200]{0:T(256)(128)(2,1)} %copy-done.5) | copy-start | bytes 1204
  318.9 30.1 %all-to-all-start.4 = ((f32[8,200,256]{2,1,0:T(8,128)}), f32[8,200,256]{2,1,0:T(8,128)S(1)}, u32[]{:S(2)}, u32[]{:S(2)}) async-start(f32[8,200,256]{2,1,0:T(8,128)} %bitcast.90), calls=%async_computation.4 | async-start | bytes 3276800 | tf_op jit(solution)/shard_map/all_to_all | solution.py:231
  326.2 89.0 %all-gather.19.cloned.1.call-start = ((), (), s32[]{:S(2)}) async-start(), calls=%async_computation.13 | async-start | bytes 1622016 | tf_op jit(solution)/shard_map/all_gather | solution.py:284
  327.6 132.2 %all-gather.15.cloned.1.call-start = ((), (), s32[]{:S(2)}) async-start(), calls=%async_computation.11 | async-start | bytes 1179648 | tf_op jit(solution)/shard_map/all_gather | solution.py:294
  462.2 12.7 %copy-start = (bf16[4,8,3072]{2,1,0:T(8,128)(2,1)S(1)}, bf16[4,8,3072]{2,1,0:T(8,128)(2,1)}, u32[]{:S(2)}) copy-start(bf16[4,8,3072]{2,1,0:T(8,128)(2,1)} %add_convert_fusion.1) | copy-start | bytes 589828
Sparse Core Ops, SparseCore 0:
  9.2 73.1 all-gather.8
  98.8 64.2 all-gather.16
  182.7 44.4 all-gather.10
  243.2 69.2 all-gather.12
  328.6 64.1 all-gather.18
  415.3 44.4 all-gather.14

commit v2 on v1

--- a/solution.py
+++ b/solution.py
@@ -39,11 +39,39 @@
     return high, (x - high.astype(F32)).astype(BF)
 
 
+def pick_barrier(peers):
+    barrier = pltpu.get_barrier_semaphore()
+    for axis, count in peers:
+        here = lax.axis_index(axis)
+
+        def greet(t, carry):
+            pl.semaphore_signal(
+                barrier,
+                inc=1,
+                device_id={axis: lax.rem(here + t, count)},
+                device_id_type=pl.DeviceIdType.MESH,
+            )
+            return carry
+
+        lax.fori_loop(1, count, greet, 0)
+    pl.semaphore_wait(barrier, sum(count - 1 for _, count in peers))
+
+
+def remote(src, dst, send_sem, recv_sem, where):
+    return pltpu.make_async_remote_copy(
+        src_ref=src,
+        dst_ref=dst,
+        send_sem=send_sem,
+        recv_sem=recv_sem,
+        device_id=where,
+        device_id_type=pl.DeviceIdType.MESH,
+    )
+
+
 def scan_kernel(
     forward,
-    s_ref,
-    d_ref,
-    r_ref,
+    shards,
+    mixed_ref,
     w1_ref,
     b1_ref,
     w2_ref,
@@ -51,6 +79,10 @@
     g_ref,
     c_ref,
     o_ref,
+    chain,
+    outs,
+    send_sem,
+    recv_sem,
     w1d,
     b1,
     w2t,
@@ -65,9 +97,62 @@
     sh_p,
     sl_p,
 ):
-    steps, size, lanes = s_ref.shape
-    hidden = w1_ref.shape[1]
-    half = lanes // 2
+    size, hidden = w1_ref.shape
+    lanes = 2 * MINI
+    half = MINI
+    parts, seqs, per, _ = mixed_ref.shape
+    copies = shards // seqs
+    per = half // per
+    minis = parts // per
+    steps = shards * minis + 1
+    index = lax.axis_index("seq")
+    lane = lax.rem(lax.axis_index("head"), copies)
+    row_here = lax.div(index, copies)
+    active = lax.rem(index, copies) == lane
+
+    pick_barrier([("seq", shards)])
+    landing = chain.at[pl.ds(index * parts, parts)]
+    sends = []
+    for t in range(1, seqs):
+        there = lax.rem(row_here + t, seqs)
+        sends.append(
+            remote(
+                mixed_ref.at[:, there],
+                landing,
+                send_sem.at[t],
+                recv_sem.at[index],
+                {"seq": there * copies + lane},
+            )
+        )
+    own = pltpu.make_async_copy(mixed_ref.at[:, row_here], landing, recv_sem.at[index])
+    across = remote(
+        mixed_ref.at[:, row_here],
+        landing,
+        send_sem.at[0],
+        recv_sem.at[index],
+        {"seq": row_here * copies + 1 - lax.rem(index, copies)},
+    )
+
+    @pl.when(active)
+    def _():
+        own.start()
+
+    @pl.when(jnp.logical_not(active))
+    def _():
+        across.start()
+
+    for copy in sends:
+        copy.start()
+
+    def place(j):
+        j = jnp.clip(j, 0, steps - 2)
+        return j if forward else steps - 2 - j
+
+    def wait_for(shard):
+        pltpu.make_async_copy(
+            mixed_ref.at[:, row_here], chain.at[pl.ds(shard * parts, parts)], recv_sem.at[shard]
+        ).wait()
+
     w1d[...] = jnp.concatenate([w1_ref[...], w1_ref[...]], 0).T
     b1[...] = jnp.broadcast_to(b1_ref[...], (lanes, hidden)).T
     centred = w2_ref[...] - jnp.mean(w2_ref[...], axis=1, keepdims=True)
@@ -82,6 +167,7 @@
     seen = (row <= col) if forward else (row >= col)
     first_mask = (seen | (col >= half)).astype(F32)
     second_mask = (~seen & (col < half)).astype(F32)
+    left = col[:size] < half
     low_half = lax.broadcasted_iota(jnp.int32, (hidden, lanes), 1) < half
     gain = jnp.broadcast_to(g_ref[...], (size, lanes))
     shift = jnp.broadcast_to(c_ref[...], (size, lanes))
@@ -96,7 +182,21 @@
         return jnp.concatenate([jnp.where(low_half, high, low), high], 1)
 
     def step(j, carry):
-        s = s_ref[j]
+        @pl.when((lax.rem(j, minis) == 0) & (j < steps - 1))
+        def _():
+            arrived = lax.div(place(j), minis)
+            wait_for(arrived)
+
+        before, now = place(j - 1), place(j)
+        old = chain[pl.ds(before * per, per)].reshape(half, 4 * size)
+        new = chain[pl.ds(now * per, per)].reshape(half, 4 * size)
+        turned = jnp.concatenate([old[:, :lanes], new[:, :lanes]], 0).T
+        s = jnp.where(left, turned[:size], turned[size:])
+        turned = jnp.concatenate([old[:, lanes:], new[:, lanes:]], 0).T
+        target = turned[:size] - s
+        rate = jnp.where(
+            left[:1], 0.0, jax.nn.sigmoid(turned[size : size + 1]) * (1.0 / HEAD_SIZE)
+        )
         sh, sl = split(s)
         shp, slp = sh_p[...], sl_p[...]
         g1h, g1l = g1h_p[...], g1l_p[...]
@@ -143,7 +243,7 @@
         )
         ch, cl = split((cross + 1.0) * second_mask)
         z2o = z2 + dot(g2s, jnp.concatenate([ch, ch, cl], 0), NN)
-        d0 = gain * (shift - d_ref[j])
+        d0 = gain * (shift - target)
         zz = z2 * z2
         s_zz = jnp.sum(zz, axis=0, keepdims=True)
         s_g = jnp.sum(gain2 * z2, axis=0, keepdims=True)
@@ -154,7 +254,7 @@
         sum_h = inv * s_g + s_d
         sum_hn = inv * (inv * s_gzz + s_dz)
         n = z2 * inv
-        scale = inv * r_ref[j]
+        scale = inv * rate
         g2h_n, g2l_n = split(scale * (gain2 * n + d0 - (sum_h + n * sum_hn) * (1.0 / size)))
         g1 = (
             dot(stacked(w2d_new), jnp.concatenate([g2h_n, g2h_n, g2l_n, blank], 0), NN) * slope
@@ -162,7 +262,8 @@
         g1h_n, g1l_n = split(g1)
         s_oo = jnp.sum(z2o * z2o, axis=0, keepdims=True)
         no = z2o * lax.rsqrt(s_oo * (1.0 / size) + EPS)
-        o_ref[j] = (s + gain * no + shift).astype(BF)
+        done = (s + gain * no + shift).T[:half].reshape(per, half // per, size)
+        outs[pl.ds(lax.rem(before, minis) * per, per), lax.div(before, minis)] = done
         g1h_p[...] = g1h_n
         g1l_p[...] = g1l_n
         g2h_p[...] = g2h_n
@@ -173,20 +274,36 @@
         sl_p[...] = sl
         return carry
 
-    lax.fori_loop(0, steps, step, 0)
-
-
-def run_scan(forward, s, d, r, w1, b1, w2, b2, g, c):
-    steps, size, lanes = s.shape
-    hidden = w1.shape[1]
+    @pl.when(active)
+    def _():
+        lax.fori_loop(0, steps, step, 0)
+        o_ref[...] = outs[...].reshape(o_ref.shape).astype(BF)
+
+    @pl.when(jnp.logical_not(active))
+    def _():
+        across.wait_send()
+
+    for copy in sends:
+        copy.wait_send()
+
+
+def run_scan(forward, number, mixed, w1, b1, w2, b2, g, c):
+    parts, seqs, rows, width = mixed.shape
+    shards = lax.axis_size("seq")
+    size, hidden = w1.shape
+    lanes = 2 * MINI
     vmem = pl.BlockSpec(memory_space=pltpu.VMEM)
     pair = lambda shape: [pltpu.VMEM(shape, BF)] * 2
     return pl.pallas_call(
-        functools.partial(scan_kernel, forward),
-        out_shape=jax.ShapeDtypeStruct((steps, size, lanes), BF),
-        in_specs=[vmem] * 9,
+        functools.partial(scan_kernel, forward, shards),
+        out_shape=jax.ShapeDtypeStruct((parts, shards * rows, size), BF),
+        in_specs=[pl.BlockSpec(memory_space=pl.ANY)] + [vmem] * 6,
         out_specs=vmem,
         scratch_shapes=[
+            pltpu.VMEM((shards * parts, rows, width), F32),
+            pltpu.VMEM((parts, shards, rows, size), F32),
+            pltpu.SemaphoreType.DMA((seqs,)),
+            pltpu.SemaphoreType.DMA((shards,)),
             pltpu.VMEM((hidden, lanes), F32),
             pltpu.VMEM((hidden, lanes), F32),
             pltpu.VMEM((size, hidden), F32),
@@ -197,53 +314,258 @@
             *pair((hidden, lanes)),
             *pair((size, lanes)),
         ],
-        compiler_params=pltpu.CompilerParams(vmem_limit_bytes=32 * 2**20),
+        compiler_params=pltpu.CompilerParams(
+            vmem_limit_bytes=40 * 2**20, collective_id=number, has_side_effects=True
+        ),
         cost_estimate=pl.CostEstimate(
-            flops=steps * 2 * 3008 * 65536, bytes_accessed=5 * steps * size * lanes * 2, transcendentals=0
+            flops=33 * 2 * 3008 * 65536, bytes_accessed=2 * 2**20, transcendentals=0
         ),
         name="scan_fwd" if forward else "scan_rev",
-    )(s, d, r, w1, b1, w2, b2, g, c)
-
-
-def assemble(chain, forward):
-    shards, rows, tokens = chain.shape
-    n = shards * tokens // MINI
-    blocks = chain.reshape(shards, rows, tokens // MINI, MINI).transpose(0, 2, 1, 3).reshape(n, rows, MINI)
-    if not forward:
-        blocks = blocks[::-1]
-    q = blocks[:, :HEAD_SIZE]
-    k = blocks[:, HEAD_SIZE : 2 * HEAD_SIZE]
-    v = blocks[:, 2 * HEAD_SIZE : 3 * HEAD_SIZE]
-    logit = blocks[:, 3 * HEAD_SIZE : 3 * HEAD_SIZE + 1]
-    before = lambda x: jnp.pad(x, ((1, 0), (0, 0), (0, 0)))
-    after = lambda x: jnp.pad(x, ((0, 1), (0, 0), (0, 0)))
-    s = jnp.concatenate([before(q), after(k)], -1)
-    d = jnp.pad(v - k, ((0, 1), (0, 0), (MINI, 0)))
-    r = jnp.pad(jax.nn.sigmoid(logit) / HEAD_SIZE, ((0, 1), (0, 0), (MINI, 0)))
-    return s, d, r
-
-
-def chain_heads(mixed, forward, params):
-    seqs = mixed.shape[0]
-    shards = lax.axis_size("seq")
+    )(mixed, w1, b1, w2, b2, g, c)
+
+
+def gather_blocks(local, full, own_sem, send_sem, recv_sem):
+    heads = full.shape[0]
+    ring = heads // 4
+    head = lax.axis_index("head")
+    x = lax.div(head, 2 * ring)
+    z = lax.rem(lax.div(head, 2), ring)
+    core = lax.rem(head, 2)
+    name = lambda x_, z_, c_: x_ * 2 * ring + lax.rem(z_ + 2 * ring, ring) * 2 + c_
+    up, down = name(x, z + 1, core), name(x, z - 1, core)
+    beside, twin = name(1 - x, z, core), name(x, z, 1 - core)
+    started = []
+
+    def send(block, part, kind, to, src=None):
+        dst = full.at[block, part]
+        copy = remote(
+            dst if src is None else src,
+            dst,
+            send_sem.at[kind, block, part],
+            recv_sem.at[block, part],
+            {"head": to},
+        )
+        copy.start()
+        started.append(copy)
+
+    def arrive(block, part):
+        pltpu.make_async_copy(
+            local.at[part], full.at[block, part], recv_sem.at[block, part]
+        ).wait()
+
+    own = pltpu.make_async_copy(local, full.at[head], own_sem)
+    own.start()
+    for kind, part, to in (
+        (2, 1, beside),
+        (0, 0, up),
+        (1, 0, down),
+        (0, 1, up),
+        (1, 1, down),
+        (2, 0, beside),
+        (3, 0, twin),
+        (3, 1, twin),
+    ):
+        send(head, part, kind, to, local.at[part])
+    other = name(1 - x, z, core)
+    arrive(other, 1)
+    send(other, 1, 0, up)
+    send(other, 1, 1, down)
+    send(other, 1, 3, twin)
+    last = ring // 2
+    turn = 1 - 2 * core
+    for k in range(1, last + 1):
+        ways = ((1, up, 0), (-1, down, 1)) if k < last else ((turn, None, 0),)
+        for sign, to, kind in ways:
+            mine, others = name(x, z - sign * k, core), name(1 - x, z - sign * k, core)
+            for block, part in ((mine, 0), (mine, 1), (others, 1)):
+                arrive(block, part)
+                if k < last - 1:
+                    send(block, part, kind, to)
+                if part == 0:
+                    send(block, 0, 2, beside)
+                send(block, part, 3, twin)
+        if k == last - 1:
+            to = name(x, z + turn, core)
+            mine, others = name(x, z - turn * k, core), name(1 - x, z - turn * k, core)
+            for block, part in ((mine, 0), (mine, 1), (others, 1)):
+                send(block, part, 0, to)
+        crossed = (0, k, -k) if k == 1 else ((k, -k) if k < last else (k,))
+        for off in crossed:
+            block = name(1 - x, z + off, core)
+            arrive(block, 0)
+            send(block, 0, 3, twin)
+
+    def from_twin(t, carry):
+        block = 2 * t + 1 - core
+        arrive(block, 0)
+        arrive(block, 1)
+        return carry
+
+    lax.fori_loop(0, heads // 2, from_twin, 0)
+    own.wait()
+    for copy in started:
+        copy.wait_send()
+
+
+def gather_sems(heads):
+    return [
+        pltpu.SemaphoreType.DMA,
+        pltpu.SemaphoreType.DMA((4, heads, 2)),
+        pltpu.SemaphoreType.DMA((heads, 2)),
+    ]
+
+
+def gather_kernel(heads, local, full, own_sem, send_sem, recv_sem):
+    pick_barrier([("head", heads)])
+    gather_blocks(local, full, own_sem, send_sem, recv_sem)
+
+
+def run_gather(local, number):
+    heads = lax.axis_size("head")
+    anyspec = pl.BlockSpec(memory_space=pl.ANY)
+    return pl.pallas_call(
+        functools.partial(gather_kernel, heads),
+        out_shape=jax.ShapeDtypeStruct((heads, *local.shape), BF),
+        in_specs=[anyspec],
+        out_specs=anyspec,
+        scratch_shapes=gather_sems(heads),
+        compiler_params=pltpu.CompilerParams(collective_id=number, has_side_effects=True),
+        name="gather_tokens",
+    )(local)
+
+
+def out_kernel(
+    heads,
+    shards,
+    seqs,
+    gathers,
+    o_ref,
+    w_ref,
+    local_ref,
+    *rest,
+):
+    result, rest = rest[0], rest[1:]
+    full = None
+    if gathers:
+        full, rest = rest[0], rest[1:]
+    blocks, joined, delta, parts, sem_a, sem_b, sem_c, sem_d, sem_e, sem_f, *gsems = rest
     copies = shards // seqs
-    send = jnp.repeat(mixed, copies, axis=0)
-    chain = lax.all_to_all(send, "seq", 0, 0, tiled=True)
-    out = run_scan(forward, *assemble(chain, forward), *params)
-    o = out[1:, :, :MINI]
-    if not forward:
-        o = o[::-1]
-    n = o.shape[0]
-    part = n // shards // copies
-    o = o.reshape(shards, copies, part, HEAD_SIZE, MINI)
-    mine = lax.dynamic_index_in_dim(o, lax.rem(lax.axis_index("seq"), copies), 1, keepdims=False)
-    return mine
-
-
-def back_to_shards(mine, seqs):
-    shards, part, size, mini = mine.shape
-    back = lax.all_to_all(mine, "seq", 0, 0, tiled=True)
-    return back.reshape(seqs, shards // seqs * part, size, mini)
+    index, head = lax.axis_index("seq"), lax.axis_index("head")
+    lane = lax.rem(index, copies)
+    row = lax.div(index, copies)
+    active = lane == lax.rem(head, copies)
+    slot = lax.div(head, copies)
+    pick_barrier([("head", heads), ("seq", shards)])
+
+    def first(t, to_do):
+        there = lax.rem(head + t, heads)
+        copy = remote(
+            o_ref.at[there], blocks.at[slot], sem_a.at[t], sem_b.at[slot], {"head": there}
+        )
+        to_do(copy)
+
+    keep = pltpu.make_async_copy(o_ref.at[head], blocks.at[slot], sem_b.at[slot])
+
+    @pl.when(active)
+    def _():
+        keep.start()
+        lax.fori_loop(1, heads, lambda t, c: (first(t, lambda copy: copy.start()), c)[1], 0)
+
+    size = blocks.shape[2]
+    count = blocks.shape[0]
+    for i in range(count):
+        pltpu.make_async_copy(o_ref.at[0], blocks.at[i], sem_b.at[i]).wait()
+    place = lane * seqs + row
+    joined[place] = jnp.concatenate([blocks[i] for i in range(count)], 1)
+
+    sends = []
+    for t in range(1, shards):
+        there = lax.rem(index + t, shards)
+        copy = remote(
+            joined.at[place], joined.at[place], sem_c.at[t], sem_d.at[place], {"seq": there}
+        )
+        copy.start()
+        sends.append(copy)
+    for t in range(1, shards):
+        source = lax.rem(index + shards - t, shards)
+        came = lax.rem(source, copies) * seqs + lax.div(source, copies)
+        pltpu.make_async_copy(joined.at[came], joined.at[came], sem_d.at[came]).wait()
+    rows = joined.shape[1]
+    inner = joined.shape[2]
+    total = sum(
+        jnp.dot(
+            joined[pl.ds(i * seqs, seqs)].reshape(seqs * rows, inner),
+            w_ref[i],
+            preferred_element_type=F32,
+        )
+        for i in range(copies)
+    )
+    delta[...] = total.reshape(delta.shape)
+
+    mine = pltpu.make_async_copy(delta.at[:, index], parts.at[index], sem_f.at[index])
+    mine.start()
+    for t in range(1, shards):
+        there = lax.rem(index + t, shards)
+        copy = remote(
+            delta.at[:, there], parts.at[index], sem_e.at[t], sem_f.at[index], {"seq": there}
+        )
+        copy.start()
+        sends.append(copy)
+    for i in range(shards):
+        pltpu.make_async_copy(delta.at[:, 0], parts.at[i], sem_f.at[i]).wait()
+    cut = parts.shape[3]
+    tokens = result.shape[0] * result.shape[1]
+    for i in range(shards):
+        columns = slice(i * cut, (i + 1) * cut)
+        summed = local_ref[:, :, columns].astype(F32) + parts[i].reshape(
+            result.shape[0], result.shape[1], cut
+        )
+        result[:, :, columns] = summed.astype(BF)
+    if gathers:
+        gather_blocks(result, full, *gsems)
+    for copy in sends:
+        copy.wait_send()
+
+    @pl.when(active)
+    def _():
+        lax.fori_loop(1, heads, lambda t, c: (first(t, lambda copy: copy.wait_send()), c)[1], 0)
+
+
+def run_out(o, sliced, local, seqs, gathers, number):
+    heads, shards = lax.axis_size("head"), lax.axis_size("seq")
+    copies = shards // seqs
+    _, rows, size = o.shape
+    cut = sliced.shape[2]
+    count = heads // copies
+    vmem = pl.BlockSpec(memory_space=pltpu.VMEM)
+    shape = jax.ShapeDtypeStruct(local.shape, BF)
+    out_shape, out_specs = [shape], [vmem]
+    if gathers:
+        out_shape.append(jax.ShapeDtypeStruct((heads, *local.shape), BF))
+        out_specs.append(pl.BlockSpec(memory_space=pl.ANY))
+    return pl.pallas_call(
+        functools.partial(out_kernel, heads, shards, seqs, gathers),
+        out_shape=out_shape,
+        in_specs=[vmem] * 3,
+        out_specs=out_specs,
+        scratch_shapes=[
+            pltpu.VMEM((count, rows, size), BF),
+            pltpu.VMEM((shards, rows, count * size), BF),
+            pltpu.VMEM((seqs, shards, rows // shards, cut), F32),
+            pltpu.VMEM((shards, seqs, rows // shards, cut), F32),
+            pltpu.SemaphoreType.DMA((heads,)),
+            pltpu.SemaphoreType.DMA((count,)),
+            pltpu.SemaphoreType.DMA((shards,)),
+            pltpu.SemaphoreType.DMA((shards,)),
+            pltpu.SemaphoreType.DMA((shards,)),
+            pltpu.SemaphoreType.DMA((shards,)),
+            *(gather_sems(heads) if gathers else []),
+        ],
+        compiler_params=pltpu.CompilerParams(
+            vmem_limit_bytes=40 * 2**20, collective_id=number, has_side_effects=True
+        ),
+        name="out_gather" if gathers else "out_last",
+    )(o, sliced, local)
 
 
 def body(
@@ -263,10 +585,16 @@
     heads = lax.axis_size("head")
     index = lax.axis_index("seq")
     cut = width // shards
+    copies = shards // seqs
 
     def weights(layer):
         return jnp.concatenate(
-            [qkv_weight[layer, 0], rate_weight[layer], jnp.zeros((7, width), BF)], 0
+            [
+                qkv_weight[layer, 0],
+                rate_weight[layer],
+                jnp.zeros((HEAD_SIZE - 1, width), BF),
+            ],
+            0,
         )
 
     def params(layer):
@@ -281,33 +609,24 @@
 
     def out_slice(layer):
         piece = lax.dynamic_slice_in_dim(out_weight[layer], index * cut, cut, 1)
-        return lax.all_gather(piece, "head", axis=0, tiled=True)
+        pieces = lax.all_gather(piece, "head", axis=0)
+        size = piece.shape[0]
+        pieces = pieces.reshape(heads // copies, copies, size, cut).transpose(1, 0, 2, 3)
+        return pieces.reshape(copies, heads // copies * size, cut)
 
     def project(layer, full):
-        return jnp.einsum("ed,bld->bel", weights(layer), full, preferred_element_type=F32)
-
-    def own_rows(o):
-        split = o.reshape(seqs, -1, HEAD_SIZE, MINI // rows_here, rows_here)
-        split = split.transpose(1, 3, 0, 4, 2).reshape(heads, seqs * rows_here, HEAD_SIZE)
-        got = lax.all_to_all(split, "head", 0, 0, tiled=True)
-        mine = got.transpose(1, 0, 2).reshape(seqs * rows_here, heads * HEAD_SIZE)
-        return lax.all_gather(mine, "seq", axis=0, tiled=True)
-
-    def layer_out(layer, local, o, sliced):
-        delta = jnp.dot(own_rows(o), sliced, preferred_element_type=F32)
-        delta = delta.reshape(shards, seqs * rows_here, cut)
-        delta = lax.all_to_all(delta, "seq", 0, 0, tiled=True)
-        delta = delta.transpose(1, 0, 2).reshape(seqs, rows_here, width)
-        return (local.astype(F32) + delta).astype(BF)
-
-    full = lax.all_gather(tokens, "head", axis=1, tiled=True)
-    mixed = project(0, full)
+        flat = full.reshape(heads * seqs * rows_here, width)
+        mixed = jnp.einsum("nd,ed->ne", flat, weights(layer), preferred_element_type=F32)
+        return mixed.reshape(heads, seqs, rows_here, 4 * HEAD_SIZE)
+
+    local = tokens.reshape(2, seqs * rows_here // 2, width)
+    full = run_gather(local, 0)
     sliced = out_slice(0), out_slice(1)
-    o = back_to_shards(chain_heads(mixed, True, params(0)), seqs)
-    middle = layer_out(0, tokens, o, sliced[0])
-    full = lax.all_gather(middle, "head", axis=1, tiled=True)
-    o = back_to_shards(chain_heads(project(1, full), False, params(1)), seqs)
-    return layer_out(1, middle, o, sliced[1])
+    o = run_scan(True, 1, project(0, full), *params(0))
+    middle, full = run_out(o, sliced[0], local, seqs, True, 2)
+    o = run_scan(False, 3, project(1, full), *params(1))
+    (result,) = run_out(o, sliced[1], middle, seqs, False, 4)
+    return result.reshape(tokens.shape)
 
 
 def solution(mesh):

time: 484 us -> 318 us (0.66)
  waiting for transfers between devices: 270 us -> 35.7 us
  Pallas kernels: 65.7 us -> 253 us
  blocking collectives: 77.8 us -> 0 us
  starting transfers between devices: 14.9 us -> 0.04 us
  local copies, waits for them, and re-layouts: 21.8 us -> 9.3 us
  matrix products: 14.9 us -> 6.54 us
    all_gather x6 -> x2, waiting for transfers between devices: 229 us -> 35.6 us  [out_slice(): pieces = lax.all_gather(piece, 'head', axis=0)]
    pallas_call x2 -> x5, Pallas kernels: 65.7 us -> 253 us  [the longest x2 112 us: run_out(): pl.pallas_call(functools.partial(out_kernel, heads, shards, seqs, gathers...]
    all_to_all x6 -> x0, blocking collectives: 77.8 us -> none  [the longest x2 30.7 us: own_rows(): got = lax.all_to_all(split, 'head', 0, 0, tiled=True)]
    all_to_all x2 -> x0, waiting for transfers between devices: 40.3 us -> none  [chain_heads(): chain = lax.all_to_all(send, 'seq', 0, 0, tiled=True)]
    all_to_all x2 -> x0, starting transfers between devices: 14.6 us -> none  [chain_heads(): chain = lax.all_to_all(send, 'seq', 0, 0, tiled=True)]
    dot_general x4 -> x2, matrix products: 14.9 us -> 6.54 us  [project(): jnp.einsum('nd,ed->ne', flat, weights(layer), preferred_element_type=F32)]
  transfers between devices with their start and end apart: 8 -> 2, of which waited for: 6 -> 1; matrix products, arithmetic and copies ran while one was open for 4% -> 3% of each run, Pallas kernels for 14% -> 28%
where the time goes in v2:
time: 318 us
  Pallas kernels  253 us (80%)
  waiting for transfers between devices  35.7 us (11%)
  between operations  13.7 us (4%)
  local copies, waits for them, and re-layouts  9.3 us (3%)
  matrix products  6.54 us (2%)
    pallas_call x2, Pallas kernels, run_out(): pl.pallas_call(functools.partial(out_kernel, heads, shards, seqs, gathers...  112 us
    pallas_call x2, Pallas kernels, run_scan(): pl.pallas_call(functools.partial(scan_kernel, forward, shards), out_shape...  96.9 us
    pallas_call x1, Pallas kernels, run_gather(): pl.pallas_call(functools.partial(gather_kernel, heads), out_shape=jax.Sha...  43.9 us
    all_gather x2, waiting for transfers between devices, out_slice(): pieces = lax.all_gather(piece, 'head', axis=0)  35.6 us
    dot_general x2, matrix products, project(): jnp.einsum('nd,ed->ne', flat, weights(layer), preferred_element_type=F32)  6.54 us
  transfers between devices with their start and end apart: 2, of which 1 were waited for; matrix products, arithmetic and copies ran while one was open for 3% of the time, Pallas kernels for 28%

profile of v2, /device:TPU:8, one launch (start us, length us, event | category | flops | bytes accessed | tf_op | source)
XLA Modules:
  0.0 317.9 jit_solution(565035424352255643)
XLA Ops:
  6.5 1.2 fusion.16
  7.7 0.6 constant_dynamic-slice_fusion.1
  8.4 0.6 constant_dynamic-slice_fusion
  9.1 43.9 %gather_tokens.1 = bf16[32,2,16,3072]{3,2,1,0:T(8,128)(2,1)} custom-call(bf16[2,16,3072]{2,1,0:T(8,128)(2,1)} %bitcast.55), custom_call_target="tpu_custom_call" | custom-call | tf_op jit(solution)/shard_map/gather_tokens/pallas_call | solution.py:426
  53.0 1.2 slice_bitcast_fusion
  54.4 4.6 %fusion.9 = f32[1024,256]{0,1:T(8,128)S(1)} fusion(bf16[1024,3072]{1,0:T(8,128)(2,1)} %bitcast.61, bf16[1,3072]{1,0:T(2,128)(2,1)S(1)} %get-tuple-element.18, bf16[192,3072]{1,0:T(8,128)(2,1)S(1)} %get-tuple-element.10, bf16[256]{0:T(256)(128)(2,1)S(1)} %pad.5.clone), kind=kOutput, calls=%fused_computation.10 | convolution fusion | flops 1615331328 | bytes 8526336 | tf_op jit(solution)/shard_map/nd,ed->ne/dot_general | solution.py:619
  59.1 0.3 copy.22
  59.4 0.5 copy-done.3
  59.9 0.1 copy.34
  60.0 0.1 copy.24.b2_ref
  60.2 0.1 copy.25.g_ref
  60.3 0.1 copy.26.c_ref
  60.4 0.1 copy.29.b2_ref
  60.5 0.1 copy.30.g_ref
  60.6 0.1 copy.31.c_ref
  60.8 44.9 %scan_fwd.1.o_ref = bf16[32,64,64]{2,1,0:T(8,128)(2,1)S(1)} custom-call(f32[32,4,8,256]{3,2,1,0:T(8,128)S(1)} %bitcast.54, f32[64,256]{1,0:T(8,128)S(1)} %get-tuple-element.16.w1_ref, f32[1,256]{1,0:T(1,128)S(1)} %get-tuple-element.20.b1_ref, f32[256,64]{1,0:T(8,128)S(1)} %bitcast.59, f32[64,1]{1,0:T(8,128)S(1)} %copy.24.b2_ref, f32[64,1]{1,0:T(8,128)S(1)} %copy.25.g_ref, ...), custom_call_target="tpu_custom_call" | custom-call | flops 13010731008 | bytes 2097152 | tf_op jit(solution)/shard_map/scan_fwd/pallas_call | solution.py:297
  105.7 1.6 copy.27
  107.3 35.6 %all-gather.5.cloned.1.call-done = bf16[32,64,384]{2,1,0:T(8,128)(2,1)} async-done(((bf16[1,64,384]{2,1,0:T(8,128)(2,1)}), bf16[32,64,384]{2,1,0:T(8,128)(2,1)}) %all-gather.5.cloned.1.call-update) | async-done | bytes 1572880 | tf_op jit(solution)/shard_map/all_gather | solution.py:612
  142.9 1.6 copy.32
  144.6 73.7 %out_gather.1 = (bf16[2,16,3072]{2,1,0:T(8,128)(2,1)S(1)}, bf16[32,2,16,3072]{3,2,1,0:T(8,128)(2,1)S(1)}) custom-call(bf16[32,64,64]{2,1,0:T(8,128)(2,1)S(1)} %scan_fwd.1.o_ref, bf16[2,1024,384]{2,1,0:T(8,128)(2,1)S(1)} %bitcast.53, bf16[2,16,3072]{2,1,0:T(8,128)(2,1)S(1)} %bitcast.56), custom_call_target="tpu_custom_call" | custom-call | tf_op jit(solution)/shard_map/out_gather/pallas_call | solution.py:546
  218.3 1.9 fusion.5.mixed_ref
  220.2 52.0 %scan_rev.1.o_ref = bf16[32,64,64]{2,1,0:T(8,128)(2,1)S(1)} custom-call(f32[32,4,8,256]{3,2,1,0:T(8,128)S(1)} %fusion.5.mixed_ref, f32[64,256]{1,0:T(8,128)S(1)} %get-tuple-element.15.w1_ref, f32[1,256]{1,0:T(1,128)S(1)} %get-tuple-element.19.b1_ref, f32[256,64]{1,0:T(8,128)S(1)} %bitcast.58, f32[64,1]{1,0:T(8,128)S(1)} %copy.29.b2_ref, ...), custom_call_target="tpu_custom_call" | custom-call | flops 13010731008 | bytes 2097152 | tf_op jit(solution)/shard_map/scan_rev/pallas_call | solution.py:297
  272.3 38.1 %out_last.1 = bf16[2,16,3072]{2,1,0:T(8,128)(2,1)S(1)} custom-call(bf16[32,64,64]{2,1,0:T(8,128)(2,1)S(1)} %scan_rev.1.o_ref, bf16[2,1024,384]{2,1,0:T(8,128)(2,1)S(1)} %bitcast.52, bf16[2,16,3072]{2,1,0:T(8,128)(2,1)S(1)} %get-tuple-element.8.local_ref), custom_call_target="tpu_custom_call" | custom-call | tf_op jit(solution)/shard_map/out_last/pallas_call | solution.py:546
  310.4 0.7 copy.37
  (34 shorter events, 0.4 us)
Async XLA Ops:
  6.5 99.2 %all-gather.3.cloned.1.call-start = ((), (), s32[]{:S(2)}) async-start(), calls=%async_computation | async-start | bytes 1622016 | tf_op jit(solution)/shard_map/all_gather | solution.py:612
  8.4 134.6 %all-gather.5.cloned.1.call-start = ((), (), s32[]{:S(2)}) async-start(), calls=%async_computation.1 | async-start | bytes 1622016 | tf_op jit(solution)/shard_map/all_gather | solution.py:612
  9.1 43.9 %copy-start.1 = (bf16[2,1,192,3072]{3,2,1,0:T(8,128)(2,1)S(1)}, bf16[2,1,192,3072]{3,2,1,0:T(8,128)(2,1)}, u32[]{:S(2)}) copy-start(bf16[2,1,192,3072]{3,2,1,0:T(8,128)(2,1)} %param.11) | copy-start | bytes 7077892
  53.0 1.2 copy-start.5
  59.0 0.9 copy-start.3
  59.0 1.0 copy-start.7
  59.0 1.1 copy-start.8
  59.0 1.2 copy-start.9
  59.1 1.7 copy-start.6
  59.1 1.7 copy-start.4
  142.9 1.6 copy-start
  144.6 73.7 %copy-start.2 = (bf16[192,3072]{1,0:T(8,128)(2,1)S(1)}, bf16[192,3072]{1,0:T(8,128)(2,1)}, u32[]{:S(2)}) copy-start(bf16[192,3072]{1,0:T(8,128)(2,1)} %get-tuple-element.9) | copy-start | bytes 3538948
Sparse Core Ops, SparseCore 0:
  9.2 67.8 all-gather.2
  79.0 63.8 all-gather.4

commit v3 on v2

--- a/solution.py
+++ b/solution.py
@@ -39,22 +39,37 @@
     return high, (x - high.astype(F32)).astype(BF)
 
 
-def pick_barrier(peers):
+def greet(peers):
     barrier = pltpu.get_barrier_semaphore()
-    for axis, count in peers:
-        here = lax.axis_index(axis)
-
-        def greet(t, carry):
-            pl.semaphore_signal(
-                barrier,
-                inc=1,
-                device_id={axis: lax.rem(here + t, count)},
-                device_id_type=pl.DeviceIdType.MESH,
-            )
-            return carry
-
-        lax.fori_loop(1, count, greet, 0)
-    pl.semaphore_wait(barrier, sum(count - 1 for _, count in peers))
+    for where in peers:
+        pl.semaphore_signal(
+            barrier, inc=1, device_id=where, device_id_type=pl.DeviceIdType.MESH
+        )
+    pl.semaphore_wait(barrier, len(peers))
+
+
+def others(axis, count):
+    here = lax.axis_index(axis)
+    return [{axis: lax.rem(here + t, count)} for t in range(1, count)]
+
+
+class Place:
+    def __init__(self, heads):
+        self.ring = heads // 4
+        self.head = lax.axis_index("head")
+        self.x = lax.div(self.head, 2 * self.ring)
+        self.z = lax.rem(lax.div(self.head, 2), self.ring)
+        self.core = lax.rem(self.head, 2)
+        self.up, self.down = self.name(self.x, self.z + 1), self.name(self.x, self.z - 1)
+        self.beside = self.name(1 - self.x, self.z)
+        self.twin = self.name(self.x, self.z, 1 - self.core)
+
+    def name(self, x, z, core=None):
+        core = self.core if core is None else core
+        return (x * self.ring + lax.rem(z + 2 * self.ring, self.ring)) * 2 + core
+
+    def near(self):
+        return [{"head": to} for to in (self.up, self.down, self.beside, self.twin)]
 
 
 def remote(src, dst, send_sem, recv_sem, where):
@@ -70,8 +85,11 @@
 
 def scan_kernel(
     forward,
+    layer,
     shards,
+    heads,
     mixed_ref,
+    weight_ref,
     w1_ref,
     b1_ref,
     w2_ref,
@@ -79,10 +97,13 @@
     g_ref,
     c_ref,
     o_ref,
+    sliced_ref,
     chain,
     outs,
     send_sem,
     recv_sem,
+    sliced_send,
+    sliced_recv,
     w1d,
     b1,
     w2t,
@@ -110,47 +131,110 @@
     row_here = lax.div(index, copies)
     active = lax.rem(index, copies) == lane
 
-    pick_barrier([("seq", shards)])
-    landing = chain.at[pl.ds(index * parts, parts)]
-    sends = []
-    for t in range(1, seqs):
-        there = lax.rem(row_here + t, seqs)
-        sends.append(
-            remote(
-                mixed_ref.at[:, there],
-                landing,
-                send_sem.at[t],
-                recv_sem.at[index],
-                {"seq": there * copies + lane},
-            )
-        )
-    own = pltpu.make_async_copy(mixed_ref.at[:, row_here], landing, recv_sem.at[index])
-    across = remote(
-        mixed_ref.at[:, row_here],
-        landing,
-        send_sem.at[0],
-        recv_sem.at[index],
-        {"seq": row_here * copies + 1 - lax.rem(index, copies)},
-    )
-
-    @pl.when(active)
-    def _():
-        own.start()
-
-    @pl.when(jnp.logical_not(active))
-    def _():
-        across.start()
-
-    for copy in sends:
-        copy.start()
+    at_head = Place(heads)
+    greet(others("seq", shards) + at_head.near())
+    twin = row_here * copies + 1 - lax.rem(index, copies)
+
+    def piece(m, there, send, where):
+        at = index * minis + m
+        return (
+            mixed_ref.at[pl.ds(m * per, per), there],
+            chain.at[pl.ds(at * per, per)],
+            send,
+            recv_sem.at[at],
+            where,
+        )
+
+    sends, crossing = [], []
+    for m in range(minis) if forward else reversed(range(minis)):
+        src, dst, sem, at, where = piece(m, row_here, send_sem.at[0, m], {"seq": twin})
+        keep, across = pltpu.make_async_copy(src, dst, at), remote(src, dst, sem, at, where)
+        pl.when(active)(keep.start)
+        pl.when(jnp.logical_not(active))(across.start)
+        crossing.append(across)
+        for t in range(1, seqs):
+            there = lax.rem(row_here + t, seqs)
+            copy = remote(*piece(m, there, send_sem.at[t, m], {"seq": there * copies + lane}))
+            copy.start()
+            sends.append(copy)
+
+    cut = sliced_ref.shape[3]
+    columns = weight_ref.at[layer, :, pl.ds(pl.multiple_of(index * cut, cut), cut)]
+    h = at_head
+    me = h.x * h.ring + h.z
+    keep = pltpu.make_async_copy(columns, sliced_ref.at[h.core, me], sliced_recv.at[h.core, me])
+    keep.start()
+
+    def pass_on(part, at, kind, to, src=None):
+        spot = sliced_ref.at[part, at]
+        return remote(
+            spot if src is None else src,
+            spot,
+            sliced_send.at[kind, part, at],
+            sliced_recv.at[part, at],
+            {"head": to},
+        )
+
+    def landed(part, at):
+        pltpu.make_async_copy(columns, sliced_ref.at[part, at], sliced_recv.at[part, at]).wait()
+
+    to_twin = pass_on(h.core, me, 3, h.twin, columns)
+    to_twin.start()
+
+    def relay():
+        begun = []
+
+        def send(*what):
+            copy = pass_on(*what)
+            copy.start()
+            begun.append(copy)
+
+        spot = lambda x, z: x * h.ring + lax.rem(z + 2 * h.ring, h.ring)
+        landed(h.core, me)
+        landed(1 - h.core, me)
+        for part, kind, to in (
+            (1, 2, h.beside),
+            (0, 0, h.up),
+            (0, 1, h.down),
+            (1, 0, h.up),
+            (1, 1, h.down),
+            (0, 2, h.beside),
+        ):
+            send(part, me, kind, to)
+        last = h.ring // 2
+        for k in range(last + 1):
+            for sign, to, kind in ((1, h.up, 0), (-1, h.down, 1)):
+                if (k == 0 or k == last) and sign < 0:
+                    continue
+                mine, other = spot(h.x, h.z - sign * k), spot(1 - h.x, h.z - sign * k)
+                for part, at in ((0, mine), (1, mine), (1, other)):
+                    if k == 0 and at is mine:
+                        continue
+                    landed(part, at)
+                    if k == 0:
+                        send(1, at, 0, h.up)
+                        send(1, at, 1, h.down)
+                    elif k < last - 1 or (k == last - 1 and sign > 0):
+                        send(part, at, kind, to)
+                    if part == 0:
+                        send(0, at, 2, h.beside)
+                    send(part, at, 3, h.twin)
+            for off in (k, -k) if 0 < k < last else (k,):
+                at = spot(1 - h.x, h.z + off)
+                landed(0, at)
+                send(0, at, 3, h.twin)
+        for copy in begun:
+            copy.wait_send()
+
+    pl.when(jnp.logical_not(active))(relay)
 
     def place(j):
         j = jnp.clip(j, 0, steps - 2)
         return j if forward else steps - 2 - j
 
-    def wait_for(shard):
+    def wait_for(at):
         pltpu.make_async_copy(
-            mixed_ref.at[:, row_here], chain.at[pl.ds(shard * parts, parts)], recv_sem.at[shard]
+            mixed_ref.at[pl.ds(0, per), row_here], chain.at[pl.ds(at * per, per)], recv_sem.at[at]
         ).wait()
 
     w1d[...] = jnp.concatenate([w1_ref[...], w1_ref[...]], 0).T
@@ -182,10 +266,9 @@
         return jnp.concatenate([jnp.where(low_half, high, low), high], 1)
 
     def step(j, carry):
-        @pl.when((lax.rem(j, minis) == 0) & (j < steps - 1))
+        @pl.when(j < steps - 1)
         def _():
-            arrived = lax.div(place(j), minis)
-            wait_for(arrived)
+            wait_for(place(j))
 
         before, now = place(j - 1), place(j)
         old = chain[pl.ds(before * per, per)].reshape(half, 4 * size)
@@ -281,29 +364,49 @@
 
     @pl.when(jnp.logical_not(active))
     def _():
-        across.wait_send()
+        for across in crossing:
+            across.wait_send()
 
     for copy in sends:
         copy.wait_send()
 
-
-def run_scan(forward, number, mixed, w1, b1, w2, b2, g, c):
+    to_twin.wait_send()
+
+    @pl.when(active)
+    def _():
+        def settle(at, carry):
+            landed(0, at)
+            landed(1, at)
+            return carry
+
+        lax.fori_loop(0, heads // 2, settle, 0)
+
+
+def run_scan(forward, layer, number, mixed, out_weight, w1, b1, w2, b2, g, c):
     parts, seqs, rows, width = mixed.shape
-    shards = lax.axis_size("seq")
+    shards, heads = lax.axis_size("seq"), lax.axis_size("head")
+    minis = parts * rows // MINI
+    copies = shards // seqs
+    cut = out_weight.shape[2] // shards
     size, hidden = w1.shape
     lanes = 2 * MINI
     vmem = pl.BlockSpec(memory_space=pltpu.VMEM)
     pair = lambda shape: [pltpu.VMEM(shape, BF)] * 2
     return pl.pallas_call(
-        functools.partial(scan_kernel, forward, shards),
-        out_shape=jax.ShapeDtypeStruct((parts, shards * rows, size), BF),
-        in_specs=[pl.BlockSpec(memory_space=pl.ANY)] + [vmem] * 6,
-        out_specs=vmem,
+        functools.partial(scan_kernel, forward, layer, shards, heads),
+        out_shape=[
+            jax.ShapeDtypeStruct((parts, shards * rows, size), BF),
+            jax.ShapeDtypeStruct((copies, heads // copies, size, cut), BF),
+        ],
+        in_specs=[pl.BlockSpec(memory_space=pl.ANY)] * 2 + [vmem] * 6,
+        out_specs=[vmem, pl.BlockSpec(memory_space=pl.ANY)],
         scratch_shapes=[
             pltpu.VMEM((shards * parts, rows, width), F32),
             pltpu.VMEM((parts, shards, rows, size), F32),
-            pltpu.SemaphoreType.DMA((seqs,)),
-            pltpu.SemaphoreType.DMA((shards,)),
+            pltpu.SemaphoreType.DMA((seqs, minis)),
+            pltpu.SemaphoreType.DMA((shards * minis,)),
+            pltpu.SemaphoreType.DMA((4, 2, heads // 2)),
+            pltpu.SemaphoreType.DMA((2, heads // 2)),
             pltpu.VMEM((hidden, lanes), F32),
             pltpu.VMEM((hidden, lanes), F32),
             pltpu.VMEM((size, hidden), F32),
@@ -321,117 +424,139 @@
             flops=33 * 2 * 3008 * 65536, bytes_accessed=2 * 2**20, transcendentals=0
         ),
         name="scan_fwd" if forward else "scan_rev",
-    )(mixed, w1, b1, w2, b2, g, c)
-
-
-def gather_blocks(local, full, own_sem, send_sem, recv_sem):
-    heads = full.shape[0]
-    ring = heads // 4
-    head = lax.axis_index("head")
-    x = lax.div(head, 2 * ring)
-    z = lax.rem(lax.div(head, 2), ring)
-    core = lax.rem(head, 2)
-    name = lambda x_, z_, c_: x_ * 2 * ring + lax.rem(z_ + 2 * ring, ring) * 2 + c_
-    up, down = name(x, z + 1, core), name(x, z - 1, core)
-    beside, twin = name(1 - x, z, core), name(x, z, 1 - core)
+    )(mixed, out_weight, w1, b1, w2, b2, g, c)
+
+
+def gather_project(layer, local, qkv_ref, rate_ref, mixed, full, weight, own_sem, send_sem, recv_sem):
+    ring = full.shape[0]
+    h = Place(4 * ring)
+    x, z, core, name = h.x, h.z, h.core, h.name
+    up, down, beside, twin = h.up, h.down, h.beside, h.twin
+    here, across = 2 * x + core, 2 * (1 - x) + core
+    last = ring // 2
     started = []
 
-    def send(block, part, kind, to, src=None):
-        dst = full.at[block, part]
+    def spot(off):
+        off = (off + last - 1) % ring - last + 1
+        return 2 * off - 1 if off > 0 else -2 * off
+
+    def send(at, which, part, kind, to, to_at=None, src=None):
+        to_at = at if to_at is None else to_at
         copy = remote(
-            dst if src is None else src,
-            dst,
-            send_sem.at[kind, block, part],
-            recv_sem.at[block, part],
+            full.at[at, which, part] if src is None else src,
+            full.at[to_at, which, part],
+            send_sem.at[kind, at, which, part],
+            recv_sem.at[to_at, which, part],
             {"head": to},
         )
         copy.start()
         started.append(copy)
 
-    def arrive(block, part):
+    def arrive(at, which, part):
         pltpu.make_async_copy(
-            local.at[part], full.at[block, part], recv_sem.at[block, part]
+            local.at[part], full.at[at, which, part], recv_sem.at[at, which, part]
         ).wait()
 
-    own = pltpu.make_async_copy(local, full.at[head], own_sem)
+    own = pltpu.make_async_copy(local, full.at[0, here], own_sem.at[0])
     own.start()
-    for kind, part, to in (
-        (2, 1, beside),
-        (0, 0, up),
-        (1, 0, down),
-        (0, 1, up),
-        (1, 1, down),
-        (2, 0, beside),
-        (3, 0, twin),
-        (3, 1, twin),
+    for kind, part, to, at in (
+        (2, 1, beside, 0),
+        (0, 0, up, spot(-1)),
+        (1, 0, down, spot(1)),
+        (0, 1, up, spot(-1)),
+        (1, 1, down, spot(1)),
+        (2, 0, beside, 0),
+        (3, 0, twin, 0),
+        (3, 1, twin, 0),
     ):
-        send(head, part, kind, to, local.at[part])
-    other = name(1 - x, z, core)
-    arrive(other, 1)
-    send(other, 1, 0, up)
-    send(other, 1, 1, down)
-    send(other, 1, 3, twin)
-    last = ring // 2
+        send(0, here, part, kind, to, at, local.at[part])
+    size = qkv_ref.shape[2]
+    load = pltpu.make_async_copy(qkv_ref.at[layer, 0], weight.at[pl.ds(0, size)], own_sem.at[1])
+    load.start()
+    weight[size:] = jnp.broadcast_to(rate_ref[layer], (weight.shape[0] - size, weight.shape[1]))
+    arrive(0, across, 1)
+    send(0, across, 1, 0, up, spot(-1))
+    send(0, across, 1, 1, down, spot(1))
+    send(0, across, 1, 3, twin)
+    arrive(0, across, 0)
+    send(0, across, 0, 3, twin)
+    load.wait()
+    own.wait()
+
+    def project(places, offsets):
+        for at in places:
+            for x_ in (0, 1):
+                arrive(at, 2 * x_ + 1 - core, 0)
+                arrive(at, 2 * x_ + 1 - core, 1)
+        count = len(places)
+        block = full[places[0] : places[0] + count]
+        rows = block.shape[1] * block.shape[2] * block.shape[3]
+        out = dot(block.reshape(count * rows, block.shape[4]), weight[...], NT)
+        out = out.reshape(count, 2, 2, *mixed.shape[1:])
+        for i, off in enumerate(offsets):
+            for x_ in (0, 1):
+                mixed[pl.ds(name(x_, z + off, 0), 2)] = out[i, x_]
+
     turn = 1 - 2 * core
     for k in range(1, last + 1):
-        ways = ((1, up, 0), (-1, down, 1)) if k < last else ((turn, None, 0),)
-        for sign, to, kind in ways:
-            mine, others = name(x, z - sign * k, core), name(1 - x, z - sign * k, core)
-            for block, part in ((mine, 0), (mine, 1), (others, 1)):
-                arrive(block, part)
+        ways = ((1, up, 0), (-1, down, 1)) if k < last else ((1, None, 0),)
+        for which, part in ((here, 0), (here, 1), (across, 1)):
+            for sign, to, kind in ways:
+                at = spot(-sign * k)
+                arrive(at, which, part)
                 if k < last - 1:
-                    send(block, part, kind, to)
+                    send(at, which, part, kind, to, spot(-sign * (k + 1)))
                 if part == 0:
-                    send(block, 0, 2, beside)
-                send(block, part, 3, twin)
+                    send(at, which, 0, 2, beside)
+                send(at, which, part, 3, twin)
         if k == last - 1:
             to = name(x, z + turn, core)
-            mine, others = name(x, z - turn * k, core), name(1 - x, z - turn * k, core)
-            for block, part in ((mine, 0), (mine, 1), (others, 1)):
-                send(block, part, 0, to)
-        crossed = (0, k, -k) if k == 1 else ((k, -k) if k < last else (k,))
-        for off in crossed:
-            block = name(1 - x, z + off, core)
-            arrive(block, 0)
-            send(block, 0, 3, twin)
-
-    def from_twin(t, carry):
-        block = 2 * t + 1 - core
-        arrive(block, 0)
-        arrive(block, 1)
-        return carry
-
-    lax.fori_loop(0, heads // 2, from_twin, 0)
-    own.wait()
+            at = spot(k) + 1 - core
+            for which, part in ((here, 0), (here, 1), (across, 1)):
+                send(at, which, part, 0, to, spot(last))
+        for off in (k, -k) if k < last else (k,):
+            arrive(spot(off), across, 0)
+            send(spot(off), across, 0, 3, twin)
+        if k == 1:
+            project((0,), (0,))
+        else:
+            project((2 * k - 3, 2 * k - 2), (k - 1, 1 - k))
+    project((2 * last - 1,), (last,))
     for copy in started:
         copy.wait_send()
 
 
-def gather_sems(heads):
+def gather_scratch(heads, width):
     return [
-        pltpu.SemaphoreType.DMA,
-        pltpu.SemaphoreType.DMA((4, heads, 2)),
-        pltpu.SemaphoreType.DMA((heads, 2)),
+        pltpu.VMEM((heads // 4, 4, 2, 16, width), BF),
+        pltpu.VMEM((4 * HEAD_SIZE, width), BF),
+        pltpu.SemaphoreType.DMA((2,)),
+        pltpu.SemaphoreType.DMA((4, heads // 4, 4, 2)),
+        pltpu.SemaphoreType.DMA((heads // 4, 4, 2)),
     ]
 
 
-def gather_kernel(heads, local, full, own_sem, send_sem, recv_sem):
-    pick_barrier([("head", heads)])
-    gather_blocks(local, full, own_sem, send_sem, recv_sem)
-
-
-def run_gather(local, number):
+def gather_kernel(heads, local, qkv_ref, rate_ref, mixed, *scratch):
+    greet(Place(heads).near())
+    gather_project(0, local, qkv_ref, rate_ref, mixed, *scratch)
+
+
+def run_gather(local, qkv_weight, rate_weight, seqs, number):
     heads = lax.axis_size("head")
+    parts, rows, width = local.shape
     anyspec = pl.BlockSpec(memory_space=pl.ANY)
+    vmem = pl.BlockSpec(memory_space=pltpu.VMEM)
     return pl.pallas_call(
         functools.partial(gather_kernel, heads),
-        out_shape=jax.ShapeDtypeStruct((heads, *local.shape), BF),
-        in_specs=[anyspec],
-        out_specs=anyspec,
-        scratch_shapes=gather_sems(heads),
-        compiler_params=pltpu.CompilerParams(collective_id=number, has_side_effects=True),
+        out_shape=jax.ShapeDtypeStruct((heads, seqs, parts * rows // seqs, 4 * HEAD_SIZE), F32),
+        in_specs=[vmem, anyspec, vmem],
+        out_specs=vmem,
+        scratch_shapes=gather_scratch(heads, width),
+        compiler_params=pltpu.CompilerParams(
+            vmem_limit_bytes=40 * 2**20, collective_id=number, has_side_effects=True
+        ),
         name="gather_tokens",
-    )(local)
+    )(local, qkv_weight, rate_weight)
 
 
 def out_kernel(
@@ -444,10 +569,10 @@
     local_ref,
     *rest,
 ):
-    result, rest = rest[0], rest[1:]
-    full = None
     if gathers:
-        full, rest = rest[0], rest[1:]
+        qkv_ref, rate_ref, result, mixed, *rest = rest
+    else:
+        result, *rest = rest
     blocks, joined, delta, parts, sem_a, sem_b, sem_c, sem_d, sem_e, sem_f, *gsems = rest
     copies = shards // seqs
     index, head = lax.axis_index("seq"), lax.axis_index("head")
@@ -455,7 +580,7 @@
     row = lax.div(index, copies)
     active = lane == lax.rem(head, copies)
     slot = lax.div(head, copies)
-    pick_barrier([("head", heads), ("seq", shards)])
+    greet(others("head", heads) + others("seq", shards))
 
     def first(t, to_do):
         there = lax.rem(head + t, heads)
@@ -495,7 +620,7 @@
     total = sum(
         jnp.dot(
             joined[pl.ds(i * seqs, seqs)].reshape(seqs * rows, inner),
-            w_ref[i],
+            w_ref[i].reshape(inner, w_ref.shape[3]),
             preferred_element_type=F32,
         )
         for i in range(copies)
@@ -522,7 +647,7 @@
         )
         result[:, :, columns] = summed.astype(BF)
     if gathers:
-        gather_blocks(result, full, *gsems)
+        gather_project(1, result, qkv_ref, rate_ref, mixed, *gsems)
     for copy in sends:
         copy.wait_send()
 
@@ -531,22 +656,25 @@
         lax.fori_loop(1, heads, lambda t, c: (first(t, lambda copy: copy.wait_send()), c)[1], 0)
 
 
-def run_out(o, sliced, local, seqs, gathers, number):
+def run_out(o, sliced, local, seqs, number, *projections):
     heads, shards = lax.axis_size("head"), lax.axis_size("seq")
     copies = shards // seqs
     _, rows, size = o.shape
-    cut = sliced.shape[2]
+    cut = sliced.shape[3]
+    gathers = len(projections) > 0
     count = heads // copies
     vmem = pl.BlockSpec(memory_space=pltpu.VMEM)
     shape = jax.ShapeDtypeStruct(local.shape, BF)
     out_shape, out_specs = [shape], [vmem]
     if gathers:
-        out_shape.append(jax.ShapeDtypeStruct((heads, *local.shape), BF))
-        out_specs.append(pl.BlockSpec(memory_space=pl.ANY))
+        out_shape.append(
+            jax.ShapeDtypeStruct((heads, seqs, rows // shards, 4 * HEAD_SIZE), F32)
+        )
+        out_specs.append(vmem)
     return pl.pallas_call(
         functools.partial(out_kernel, heads, shards, seqs, gathers),
         out_shape=out_shape,
-        in_specs=[vmem] * 3,
+        in_specs=[vmem] * 3 + [pl.BlockSpec(memory_space=pl.ANY), vmem][: len(projections)],
         out_specs=out_specs,
         scratch_shapes=[
             pltpu.VMEM((count, rows, size), BF),
@@ -559,13 +687,13 @@
             pltpu.SemaphoreType.DMA((shards,)),
             pltpu.SemaphoreType.DMA((shards,)),
             pltpu.SemaphoreType.DMA((shards,)),
-            *(gather_sems(heads) if gathers else []),
+            *(gather_scratch(heads, local.shape[2]) if gathers else []),
         ],
         compiler_params=pltpu.CompilerParams(
             vmem_limit_bytes=40 * 2**20, collective_id=number, has_side_effects=True
         ),
         name="out_gather" if gathers else "out_last",
-    )(o, sliced, local)
+    )(o, sliced, local, *projections)
 
 
 def body(
@@ -581,21 +709,8 @@
     out_weight,
 ):
     seqs, rows_here, width = tokens.shape
-    shards = lax.axis_size("seq")
-    heads = lax.axis_size("head")
-    index = lax.axis_index("seq")
-    cut = width // shards
-    copies = shards // seqs
-
-    def weights(layer):
-        return jnp.concatenate(
-            [
-                qkv_weight[layer, 0],
-                rate_weight[layer],
-                jnp.zeros((HEAD_SIZE - 1, width), BF),
-            ],
-            0,
-        )
+    local = tokens.reshape(2, seqs * rows_here // 2, width)
+    project = (qkv_weight, rate_weight)
 
     def params(layer):
         return (
@@ -607,25 +722,11 @@
             norm_bias[layer].T,
         )
 
-    def out_slice(layer):
-        piece = lax.dynamic_slice_in_dim(out_weight[layer], index * cut, cut, 1)
-        pieces = lax.all_gather(piece, "head", axis=0)
-        size = piece.shape[0]
-        pieces = pieces.reshape(heads // copies, copies, size, cut).transpose(1, 0, 2, 3)
-        return pieces.reshape(copies, heads // copies * size, cut)
-
-    def project(layer, full):
-        flat = full.reshape(heads * seqs * rows_here, width)
-        mixed = jnp.einsum("nd,ed->ne", flat, weights(layer), preferred_element_type=F32)
-        return mixed.reshape(heads, seqs, rows_here, 4 * HEAD_SIZE)
-
-    local = tokens.reshape(2, seqs * rows_here // 2, width)
-    full = run_gather(local, 0)
-    sliced = out_slice(0), out_slice(1)
-    o = run_scan(True, 1, project(0, full), *params(0))
-    middle, full = run_out(o, sliced[0], local, seqs, True, 2)
-    o = run_scan(False, 3, project(1, full), *params(1))
-    (result,) = run_out(o, sliced[1], middle, seqs, False, 4)
+    mixed = run_gather(local, *project, seqs, 0)
+    o, sliced = run_scan(True, 0, 1, mixed, out_weight, *params(0))
+    middle, mixed = run_out(o, sliced, local, seqs, 2, *project)
+    o, sliced = run_scan(False, 1, 3, mixed, out_weight, *params(1))
+    (result,) = run_out(o, sliced, middle, seqs, 4)
     return result.reshape(tokens.shape)
 
 

time: 318 us -> 258 us (0.81)
  waiting for transfers between devices: 35.7 us -> 0 us
  between operations: 13.7 us -> 0.2 us
  matrix products: 6.54 us -> 0 us
  local copies, waits for them, and re-layouts: 9.3 us -> 4.83 us
    all_gather x2 -> x0, waiting for transfers between devices: 35.6 us -> none  [out_slice(): pieces = lax.all_gather(piece, 'head', axis=0)]
    dot_general x2 -> x0, matrix products: 6.54 us -> none  [project(): jnp.einsum('nd,ed->ne', flat, weights(layer), preferred_element_type=F32)]
    pallas_call x2, Pallas kernels: 96.9 us -> 102 us  [run_scan(): pl.pallas_call(functools.partial(scan_kernel, forward, layer, shards, hea...]
    pallas_call x1, Pallas kernels: 43.9 us -> 40.4 us  [run_gather(): pl.pallas_call(functools.partial(gather_kernel, heads), out_shape=jax.Sha...]
    reshape x2 -> x0, local copies, waits for them, and re-layouts: 3.21 us -> none  [out_slice(): pieces.reshape(heads // copies, copies, size, cut).transpose(1, 0, 2, 3)]
  transfers between devices with their start and end apart: 2 -> 0, of which waited for: 1 -> 0; matrix products, arithmetic and copies ran while one was open for 3% -> 0% of each run, Pallas kernels for 28% -> 0%
where the time goes in v3:
time: 258 us; the launch traced here: 257 us
  Pallas kernels  252 us (98%)
  local copies, waits for them, and re-layouts  4.83 us (2%)
    pallas_call x2, Pallas kernels, run_out(): pl.pallas_call(functools.partial(out_kernel, heads, shards, seqs, gathers...  109 us
    pallas_call x2, Pallas kernels, run_scan(): pl.pallas_call(functools.partial(scan_kernel, forward, layer, shards, hea...  102 us
    pallas_call x1, Pallas kernels, run_gather(): pl.pallas_call(functools.partial(gather_kernel, heads), out_shape=jax.Sha...  40.4 us

profile of v3, /device:TPU:8, one launch (start us, length us, event | category | flops | bytes accessed | tf_op | source)
XLA Modules:
  0.0 257.0 jit_solution(1859278797840671139)
XLA Ops:
  0.0 0.7 copy.11.rate_ref.rest_1_
  0.7 0.0 copy-start
  0.7 1.7 copy-done
  2.4 0.9 copy-done.2
  3.3 0.0 copy-start.10
  3.3 0.0 copy-start.7
  3.4 0.0 copy-start.4
  3.4 40.4 %gather_tokens.1.mixed_ref = f32[32,4,8,256]{3,2,1,0:T(8,128)S(1)} custom-call(bf16[2,16,3072]{2,1,0:T(8,128)(2,1)S(1)} %bitcast.24, bf16[2,1,192,3072]{3,2,1,0:T(8,128)(2,1)S(1)} %copy-done, bf16[2,1,3072]{2,1,0:T(2,128)(2,1)S(1)} %copy.11.rate_ref.rest_1_), custom_call_target="tpu_custom_call" | custom-call | tf_op jit(solution)/shard_map/gather_tokens/pallas_call | solution.py:549
  43.8 0.0 copy-done.5
  43.8 0.1 copy.21
  44.0 0.1 copy.13.b2_ref
  44.1 0.1 copy.14.g_ref
  44.2 0.1 copy.15.c_ref
  44.3 0.0 copy-start.1
  44.3 0.0 copy-start.3
  44.3 50.2 %scan_fwd.1 = (bf16[32,64,64]{2,1,0:T(8,128)(2,1)S(1)}, bf16[2,16,64,384]{3,2,1,0:T(8,128)(2,1)S(1)}) custom-call(f32[32,4,8,256]{3,2,1,0:T(8,128)S(1)} %gather_tokens.1.mixed_ref, bf16[2,64,3072]{2,1,0:T(8,128)(2,1)S(1)} %copy-done.4, f32[64,256]{1,0:T(8,128)S(1)} %get-tuple-element.20.w1_ref, f32[1,256]{1,0:T(1,128)S(1)} %get-tuple-element.22.b1_ref, ...), custom_call_target="tpu_custom_call" | custom-call | flops 13010731008 | bytes 2097152 | tf_op jit(solution)/shard_map/scan_fwd/pallas_call | solution.py:395
  94.5 73.6 %out_gather.1 = (bf16[2,16,3072]{2,1,0:T(8,128)(2,1)S(1)}, f32[32,4,8,256]{3,2,1,0:T(8,128)S(1)}) custom-call(bf16[32,64,64]{2,1,0:T(8,128)(2,1)S(1)} %get-tuple-element.11.o_ref, bf16[2,16,64,384]{3,2,1,0:T(8,128)(2,1)S(1)} %get-tuple-element.12.w_ref, bf16[2,16,3072]{2,1,0:T(8,128)(2,1)S(1)} %bitcast.25, bf16[2,1,192,3072]{3,2,1,0:T(8,128)(2,1)S(1)} %copy-done.1, ...), custom_call_target="tpu_custom_call" | custom-call | tf_op jit(solution)/shard_map/out_gather/pallas_call | solution.py:674
  168.1 0.1 copy.22
  168.2 0.1 copy.18.b2_ref
  168.3 0.1 copy.19.g_ref
  168.4 0.1 copy.20.c_ref
  168.5 52.1 %scan_rev.1 = (bf16[32,64,64]{2,1,0:T(8,128)(2,1)S(1)}, bf16[2,16,64,384]{3,2,1,0:T(8,128)(2,1)S(1)}) custom-call(f32[32,4,8,256]{3,2,1,0:T(8,128)S(1)} %get-tuple-element.13.mixed_ref, bf16[2,64,3072]{2,1,0:T(8,128)(2,1)S(1)} %copy-done.4, f32[64,256]{1,0:T(8,128)S(1)} %get-tuple-element.19.w1_ref, f32[1,256]{1,0:T(1,128)S(1)} %get-tuple-element.21.b1_ref, ...), custom_call_target="tpu_custom_call" | custom-call | flops 13010731008 | bytes 2097152 | tf_op jit(solution)/shard_map/scan_rev/pallas_call | solution.py:395
  220.6 35.7 %out_last.1 = bf16[2,16,3072]{2,1,0:T(8,128)(2,1)S(1)} custom-call(bf16[32,64,64]{2,1,0:T(8,128)(2,1)S(1)} %get-tuple-element.14.o_ref, bf16[2,16,64,384]{3,2,1,0:T(8,128)(2,1)S(1)} %get-tuple-element.15.w_ref, bf16[2,16,3072]{2,1,0:T(8,128)(2,1)S(1)} %get-tuple-element.16.local_ref), custom_call_target="tpu_custom_call" | custom-call | tf_op jit(solution)/shard_map/out_last/pallas_call | solution.py:674
  256.3 0.7 copy.24
  (19 shorter events, 0.1 us)
Async XLA Ops:
  0.7 1.7 copy-start
  2.4 0.9 copy-start.2
  3.3 40.5 %copy-start.5 = (f32[2,1,256,64]{2,3,1,0:T(8,128)S(1)}, f32[2,1,256,64]{2,3,1,0:T(8,128)}, u32[]{:S(2)}) copy-start(f32[2,1,256,64]{2,3,1,0:T(8,128)} %param.15) | copy-start | bytes 393220
  3.3 40.6 %copy-start.6 = (f32[2,1,64,256]{3,2,1,0:T(8,128)S(1)}, f32[2,1,64,256]{3,2,1,0:T(8,128)}, u32[]{:S(2)}) copy-start(f32[2,1,64,256]{3,2,1,0:T(8,128)} %param.13) | copy-start | bytes 393220
  3.3 40.6 %copy-start.8 = (f32[2,1,64]{2,1,0:T(1,128)S(1)}, f32[2,1,64]{2,1,0:T(1,128)}, u32[]{:S(2)}) copy-start(f32[2,1,64]{2,1,0:T(1,128)} %param.16) | copy-start | bytes 1540
  3.3 40.8 %copy-start.9 = (f32[2,1,64]{2,1,0:T(1,128)S(1)}, f32[2,1,64]{2,1,0:T(1,128)}, u32[]{:S(2)}) copy-start(f32[2,1,64]{2,1,0:T(1,128)} %param.17) | copy-start | bytes 1540
  3.3 40.9 %copy-start.10 = (f32[2,1,64]{2,1,0:T(1,128)S(1)}, f32[2,1,64]{2,1,0:T(1,128)}, u32[]{:S(2)}) copy-start(f32[2,1,64]{2,1,0:T(1,128)} %param.18) | copy-start | bytes 1540
  3.3 41.0 %copy-start.7 = (f32[2,1,256]{2,1,0:T(1,128)S(1)}, f32[2,1,256]{2,1,0:T(1,128)}, u32[]{:S(2)}) copy-start(f32[2,1,256]{2,1,0:T(1,128)} %param.14) | copy-start | bytes 6148
  3.4 41.0 %copy-start.4 = (bf16[2,64,3072]{2,1,0:T(8,128)(2,1)S(1)}, bf16[2,64,3072]{2,1,0:T(8,128)(2,1)}, u32[]{:S(2)}) copy-start(bf16[2,64,3072]{2,1,0:T(8,128)(2,1)} %weight_ref.3) | copy-start | bytes 2359300
  44.3 50.2 %copy-start.1 = (bf16[2,1,192,3072]{3,2,1,0:T(8,128)(2,1)S(1)}, bf16[2,1,192,3072]{3,2,1,0:T(8,128)(2,1)}, u32[]{:S(2)}) copy-start(bf16[2,1,192,3072]{3,2,1,0:T(8,128)(2,1)} %rest_0_.1) | copy-start | bytes 7077892
  44.3 50.2 %copy-start.3 = (bf16[4,8,3072]{2,1,0:T(8,128)(2,1)S(1)}, bf16[4,8,3072]{2,1,0:T(8,128)(2,1)}, u32[]{:S(2)}) copy-start(bf16[4,8,3072]{2,1,0:T(8,128)(2,1)} %param.10) | copy-start | bytes 589828

commit v4 on v3

--- a/solution.py
+++ b/solution.py
@@ -83,7 +83,7 @@
     )
 
 
-def scan_kernel(
+def scan_phase(
     forward,
     layer,
     shards,
@@ -118,7 +118,7 @@
     sh_p,
     sl_p,
 ):
-    size, hidden = w1_ref.shape
+    size, hidden = w1_ref.shape[2:]
     lanes = 2 * MINI
     half = MINI
     parts, seqs, per, _ = mixed_ref.shape
@@ -132,7 +132,6 @@
     active = lax.rem(index, copies) == lane
 
     at_head = Place(heads)
-    greet(others("seq", shards) + at_head.near())
     twin = row_here * copies + 1 - lax.rem(index, copies)
 
     def piece(m, there, send, where):
@@ -145,18 +144,32 @@
             where,
         )
 
-    sends, crossing = [], []
+    sends, keeps, crossing = [], [], []
     for m in range(minis) if forward else reversed(range(minis)):
         src, dst, sem, at, where = piece(m, row_here, send_sem.at[0, m], {"seq": twin})
-        keep, across = pltpu.make_async_copy(src, dst, at), remote(src, dst, sem, at, where)
-        pl.when(active)(keep.start)
-        pl.when(jnp.logical_not(active))(across.start)
-        crossing.append(across)
+        keeps.append(pltpu.make_async_copy(src, dst, at))
+        crossing.append(remote(src, dst, sem, at, where))
         for t in range(1, seqs):
             there = lax.rem(row_here + t, seqs)
-            copy = remote(*piece(m, there, send_sem.at[t, m], {"seq": there * copies + lane}))
+            sends.append(
+                remote(*piece(m, there, send_sem.at[t, m], {"seq": there * copies + lane}))
+            )
+
+    turn = index if forward else shards - 1 - index
+    release = jnp.maximum(2 * turn - 2, 0)
+
+    def send_all():
+        for m in range(minis):
+            pl.when(jnp.logical_not(active))(crossing[m].start)
+            for copy in sends[m * (seqs - 1) : (m + 1) * (seqs - 1)]:
+                copy.start()
+
+    @pl.when(active)
+    def _():
+        for copy in keeps:
             copy.start()
-            sends.append(copy)
+
+    pl.when(release == 0)(send_all)
 
     cut = sliced_ref.shape[3]
     columns = weight_ref.at[layer, :, pl.ds(pl.multiple_of(index * cut, cut), cut)]
@@ -203,6 +216,10 @@
             send(part, me, kind, to)
         last = h.ring // 2
         for k in range(last + 1):
+            if k == 1:
+                pl.when((release > 0) & (release <= 4))(send_all)
+            if k == 2:
+                pl.when(release > 4)(send_all)
             for sign, to, kind in ((1, h.up, 0), (-1, h.down, 1)):
                 if (k == 0 or k == last) and sign < 0:
                     continue
@@ -237,12 +254,14 @@
             mixed_ref.at[pl.ds(0, per), row_here], chain.at[pl.ds(at * per, per)], recv_sem.at[at]
         ).wait()
 
-    w1d[...] = jnp.concatenate([w1_ref[...], w1_ref[...]], 0).T
-    b1[...] = jnp.broadcast_to(b1_ref[...], (lanes, hidden)).T
-    centred = w2_ref[...] - jnp.mean(w2_ref[...], axis=1, keepdims=True)
-    w2d[...] = jnp.concatenate([centred, centred], 1)
-    w2t[...] = centred.T
-    b2[...] = jnp.broadcast_to(b2_ref[...] - jnp.mean(b2_ref[...]), (size, lanes))
+    column = lambda ref: jnp.broadcast_to(ref[layer], (lanes, ref.shape[2])).T
+    w1d[...] = jnp.concatenate([w1_ref[layer, 0], w1_ref[layer, 0]], 0).T
+    b1[...] = column(b1_ref)
+    centred = w2_ref[layer, 0] - jnp.mean(w2_ref[layer, 0], axis=0, keepdims=True)
+    w2d[...] = jnp.concatenate([centred, centred], 0).T
+    w2t[...] = centred
+    bias = column(b2_ref)
+    b2[...] = bias - jnp.mean(bias, axis=0, keepdims=True)
     for ref in (g1h_p, g1l_p, g2h_p, g2l_p, th_p, tl_p, sh_p, sl_p):
         ref[...] = jnp.zeros_like(ref)
 
@@ -253,8 +272,7 @@
     second_mask = (~seen & (col < half)).astype(F32)
     left = col[:size] < half
     low_half = lax.broadcasted_iota(jnp.int32, (hidden, lanes), 1) < half
-    gain = jnp.broadcast_to(g_ref[...], (size, lanes))
-    shift = jnp.broadcast_to(c_ref[...], (size, lanes))
+    gain, shift = column(g_ref), column(c_ref)
     gain2 = gain * gain
     ones = jnp.ones((lanes, lanes), BF)
     zeros = jnp.zeros((lanes, lanes), BF)
@@ -266,6 +284,8 @@
         return jnp.concatenate([jnp.where(low_half, high, low), high], 1)
 
     def step(j, carry):
+        pl.when((j == release) & (j > 0))(send_all)
+
         @pl.when(j < steps - 1)
         def _():
             wait_for(place(j))
@@ -380,51 +400,6 @@
             return carry
 
         lax.fori_loop(0, heads // 2, settle, 0)
-
-
-def run_scan(forward, layer, number, mixed, out_weight, w1, b1, w2, b2, g, c):
-    parts, seqs, rows, width = mixed.shape
-    shards, heads = lax.axis_size("seq"), lax.axis_size("head")
-    minis = parts * rows // MINI
-    copies = shards // seqs
-    cut = out_weight.shape[2] // shards
-    size, hidden = w1.shape
-    lanes = 2 * MINI
-    vmem = pl.BlockSpec(memory_space=pltpu.VMEM)
-    pair = lambda shape: [pltpu.VMEM(shape, BF)] * 2
-    return pl.pallas_call(
-        functools.partial(scan_kernel, forward, layer, shards, heads),
-        out_shape=[
-            jax.ShapeDtypeStruct((parts, shards * rows, size), BF),
-            jax.ShapeDtypeStruct((copies, heads // copies, size, cut), BF),
-        ],
-        in_specs=[pl.BlockSpec(memory_space=pl.ANY)] * 2 + [vmem] * 6,
-        out_specs=[vmem, pl.BlockSpec(memory_space=pl.ANY)],
-        scratch_shapes=[
-            pltpu.VMEM((shards * parts, rows, width), F32),
-            pltpu.VMEM((parts, shards, rows, size), F32),
-            pltpu.SemaphoreType.DMA((seqs, minis)),
-            pltpu.SemaphoreType.DMA((shards * minis,)),
-            pltpu.SemaphoreType.DMA((4, 2, heads // 2)),
-            pltpu.SemaphoreType.DMA((2, heads // 2)),
-            pltpu.VMEM((hidden, lanes), F32),
-            pltpu.VMEM((hidden, lanes), F32),
-            pltpu.VMEM((size, hidden), F32),
-            pltpu.VMEM((hidden, lanes), F32),
-            pltpu.VMEM((size, lanes), F32),
-            *pair((hidden, lanes)),
-            *pair((size, lanes)),
-            *pair((hidden, lanes)),
-            *pair((size, lanes)),
-        ],
-        compiler_params=pltpu.CompilerParams(
-            vmem_limit_bytes=40 * 2**20, collective_id=number, has_side_effects=True
-        ),
-        cost_estimate=pl.CostEstimate(
-            flops=33 * 2 * 3008 * 65536, bytes_accessed=2 * 2**20, transcendentals=0
-        ),
-        name="scan_fwd" if forward else "scan_rev",
-    )(mixed, out_weight, w1, b1, w2, b2, g, c)
 
 
 def gather_project(layer, local, qkv_ref, rate_ref, mixed, full, weight, own_sem, send_sem, recv_sem):
@@ -497,6 +472,19 @@
             for x_ in (0, 1):
                 mixed[pl.ds(name(x_, z + off, 0), 2)] = out[i, x_]
 
+    def hand_over(k):
+        for off in (k, -k) if k < last else (k,):
+            arrive(spot(off), across, 0)
+            send(spot(off), across, 0, 3, twin)
+
+    def project_at(k):
+        if k == 1:
+            project((0,), (0,))
+        if k < last:
+            project((2 * k - 1, 2 * k), (k, -k))
+        else:
+            project((2 * k - 1,), (k,))
+
     turn = 1 - 2 * core
     for k in range(1, last + 1):
         ways = ((1, up, 0), (-1, down, 1)) if k < last else ((1, None, 0),)
@@ -514,73 +502,42 @@
             at = spot(k) + 1 - core
             for which, part in ((here, 0), (here, 1), (across, 1)):
                 send(at, which, part, 0, to, spot(last))
-        for off in (k, -k) if k < last else (k,):
-            arrive(spot(off), across, 0)
-            send(spot(off), across, 0, 3, twin)
-        if k == 1:
-            project((0,), (0,))
-        else:
-            project((2 * k - 3, 2 * k - 2), (k - 1, 1 - k))
-    project((2 * last - 1,), (last,))
+        if k > 1:
+            hand_over(k - 1)
+        if k > 2:
+            project_at(k - 2)
+    hand_over(last)
+    project_at(last - 1)
+    project_at(last)
     for copy in started:
         copy.wait_send()
 
 
-def gather_scratch(heads, width):
-    return [
-        pltpu.VMEM((heads // 4, 4, 2, 16, width), BF),
-        pltpu.VMEM((4 * HEAD_SIZE, width), BF),
-        pltpu.SemaphoreType.DMA((2,)),
-        pltpu.SemaphoreType.DMA((4, heads // 4, 4, 2)),
-        pltpu.SemaphoreType.DMA((heads // 4, 4, 2)),
-    ]
-
-
-def gather_kernel(heads, local, qkv_ref, rate_ref, mixed, *scratch):
-    greet(Place(heads).near())
-    gather_project(0, local, qkv_ref, rate_ref, mixed, *scratch)
-
-
-def run_gather(local, qkv_weight, rate_weight, seqs, number):
-    heads = lax.axis_size("head")
-    parts, rows, width = local.shape
-    anyspec = pl.BlockSpec(memory_space=pl.ANY)
-    vmem = pl.BlockSpec(memory_space=pltpu.VMEM)
-    return pl.pallas_call(
-        functools.partial(gather_kernel, heads),
-        out_shape=jax.ShapeDtypeStruct((heads, seqs, parts * rows // seqs, 4 * HEAD_SIZE), F32),
-        in_specs=[vmem, anyspec, vmem],
-        out_specs=vmem,
-        scratch_shapes=gather_scratch(heads, width),
-        compiler_params=pltpu.CompilerParams(
-            vmem_limit_bytes=40 * 2**20, collective_id=number, has_side_effects=True
-        ),
-        name="gather_tokens",
-    )(local, qkv_weight, rate_weight)
-
-
-def out_kernel(
+def out_phase(
     heads,
     shards,
     seqs,
-    gathers,
     o_ref,
     w_ref,
     local_ref,
-    *rest,
+    result,
+    blocks,
+    joined,
+    delta,
+    parts,
+    sem_a,
+    sem_b,
+    sem_c,
+    sem_d,
+    sem_e,
+    sem_f,
 ):
-    if gathers:
-        qkv_ref, rate_ref, result, mixed, *rest = rest
-    else:
-        result, *rest = rest
-    blocks, joined, delta, parts, sem_a, sem_b, sem_c, sem_d, sem_e, sem_f, *gsems = rest
     copies = shards // seqs
     index, head = lax.axis_index("seq"), lax.axis_index("head")
     lane = lax.rem(index, copies)
     row = lax.div(index, copies)
     active = lane == lax.rem(head, copies)
     slot = lax.div(head, copies)
-    greet(others("head", heads) + others("seq", shards))
 
     def first(t, to_do):
         there = lax.rem(head + t, heads)
@@ -646,8 +603,6 @@
             result.shape[0], result.shape[1], cut
         )
         result[:, :, columns] = summed.astype(BF)
-    if gathers:
-        gather_project(1, result, qkv_ref, rate_ref, mixed, *gsems)
     for copy in sends:
         copy.wait_send()
 
@@ -656,77 +611,132 @@
         lax.fori_loop(1, heads, lambda t, c: (first(t, lambda copy: copy.wait_send()), c)[1], 0)
 
 
-def run_out(o, sliced, local, seqs, number, *projections):
+def whole_kernel(heads, shards, seqs, counts, *refs):
+    local, qkv_ref, rate_ref, weight_ref, *params = refs[:10]
+    result = refs[10]
+    rest = list(refs[11:])
+
+    def take(count):
+        taken = rest[:count]
+        del rest[:count]
+        return taken
+
+    weight, outs, middle, load_sem = take(4)
+    held = take(len(params))
+    state = take(counts[0])
+    loads = [
+        pltpu.make_async_copy(src, dst, load_sem.at[i])
+        for i, (src, dst) in enumerate(zip(params, held))
+    ]
+    for load in loads:
+        load.start()
+    greet(others("head", heads) + others("seq", shards))
+    for layer in range(2):
+        mixed, *gather = take(counts[1])
+        sliced, o, *scan = take(counts[2])
+        out = take(counts[3])
+        source, target = (local, middle) if layer == 0 else (middle, result)
+        full, *sems = gather
+        gather_project(layer, source, qkv_ref, rate_ref, mixed, full, weight, *sems)
+        chain, *scan_sems = scan
+        if layer == 0:
+            for load in loads:
+                load.wait()
+        scan_phase(
+            layer == 0,
+            layer,
+            shards,
+            heads,
+            mixed,
+            weight_ref,
+            *held,
+            o,
+            sliced,
+            chain,
+            outs,
+            *scan_sems,
+            *state,
+        )
+        out_phase(heads, shards, seqs, o, sliced, source, target, *out)
+
+
+def body(tokens, qkv_weight, rate_weight, *rest):
+    *params, out_weight = rest
+    seqs, rows, width = tokens.shape
     heads, shards = lax.axis_size("head"), lax.axis_size("seq")
+    hidden = params[0].shape[3]
+    size = HEAD_SIZE
+    lanes = 2 * MINI
     copies = shards // seqs
-    _, rows, size = o.shape
-    cut = sliced.shape[3]
-    gathers = len(projections) > 0
+    minis = heads * rows // MINI
+    cut = width // shards
     count = heads // copies
+    dma = pltpu.SemaphoreType.DMA
+    pair = lambda shape: [pltpu.VMEM(shape, BF)] * 2
+    local = tokens.reshape(2, seqs * rows // 2, width)
+    params[2] = params[2].transpose(0, 1, 3, 2)
+    state = [
+        pltpu.VMEM((hidden, lanes), F32),
+        pltpu.VMEM((hidden, lanes), F32),
+        pltpu.VMEM((size, hidden), F32),
+        pltpu.VMEM((hidden, lanes), F32),
+        pltpu.VMEM((size, lanes), F32),
+        *pair((hidden, lanes)),
+        *pair((size, lanes)),
+        *pair((hidden, lanes)),
+        *pair((size, lanes)),
+    ]
+    gather = [
+        pltpu.VMEM((heads, seqs, rows, 4 * size), F32),
+        pltpu.VMEM((heads // 4, 4, *local.shape), BF),
+        dma((2,)),
+        dma((4, heads // 4, 4, 2)),
+        dma((heads // 4, 4, 2)),
+    ]
+    scan = [
+        pltpu.VMEM((copies, count, size, cut), BF),
+        pltpu.VMEM((heads, shards * rows, size), BF),
+        pltpu.VMEM((shards * heads, rows, 4 * size), F32),
+        dma((seqs, minis)),
+        dma((shards * minis,)),
+        dma((4, 2, count)),
+        dma((2, count)),
+    ]
+    out = [
+        pltpu.VMEM((count, shards * rows, size), BF),
+        pltpu.VMEM((shards, shards * rows, count * size), BF),
+        pltpu.VMEM((seqs, shards, rows, cut), F32),
+        pltpu.VMEM((shards, seqs, rows, cut), F32),
+        dma((heads,)),
+        dma((count,)),
+        dma((shards,)),
+        dma((shards,)),
+        dma((shards,)),
+        dma((shards,)),
+    ]
+    hbm = pl.BlockSpec(memory_space=pltpu.HBM)
     vmem = pl.BlockSpec(memory_space=pltpu.VMEM)
-    shape = jax.ShapeDtypeStruct(local.shape, BF)
-    out_shape, out_specs = [shape], [vmem]
-    if gathers:
-        out_shape.append(
-            jax.ShapeDtypeStruct((heads, seqs, rows // shards, 4 * HEAD_SIZE), F32)
-        )
-        out_specs.append(vmem)
-    return pl.pallas_call(
-        functools.partial(out_kernel, heads, shards, seqs, gathers),
-        out_shape=out_shape,
-        in_specs=[vmem] * 3 + [pl.BlockSpec(memory_space=pl.ANY), vmem][: len(projections)],
-        out_specs=out_specs,
+    counts = (len(state), len(gather), len(scan), len(out))
+    result = pl.pallas_call(
+        functools.partial(whole_kernel, heads, shards, seqs, counts),
+        out_shape=jax.ShapeDtypeStruct(local.shape, BF),
+        in_specs=[vmem, hbm, vmem, hbm] + [hbm] * 6,
+        out_specs=vmem,
         scratch_shapes=[
-            pltpu.VMEM((count, rows, size), BF),
-            pltpu.VMEM((shards, rows, count * size), BF),
-            pltpu.VMEM((seqs, shards, rows // shards, cut), F32),
-            pltpu.VMEM((shards, seqs, rows // shards, cut), F32),
-            pltpu.SemaphoreType.DMA((heads,)),
-            pltpu.SemaphoreType.DMA((count,)),
-            pltpu.SemaphoreType.DMA((shards,)),
-            pltpu.SemaphoreType.DMA((shards,)),
-            pltpu.SemaphoreType.DMA((shards,)),
-            pltpu.SemaphoreType.DMA((shards,)),
-            *(gather_scratch(heads, local.shape[2]) if gathers else []),
+            pltpu.VMEM((4 * size, width), BF),
+            pltpu.VMEM((heads, shards, rows, size), F32),
+            pltpu.VMEM(local.shape, BF),
+            dma((len(params),)),
+            *[pltpu.VMEM(param.shape, F32) for param in params],
+            *state,
+            *(gather + scan + out),
+            *(gather + scan + out),
         ],
         compiler_params=pltpu.CompilerParams(
-            vmem_limit_bytes=40 * 2**20, collective_id=number, has_side_effects=True
+            vmem_limit_bytes=63 * 2**20, collective_id=0, has_side_effects=True
         ),
-        name="out_gather" if gathers else "out_last",
-    )(o, sliced, local, *projections)
-
-
-def body(
-    tokens,
-    qkv_weight,
-    rate_weight,
-    first_init,
-    first_bias,
-    second_init,
-    second_bias,
-    norm_gain,
-    norm_bias,
-    out_weight,
-):
-    seqs, rows_here, width = tokens.shape
-    local = tokens.reshape(2, seqs * rows_here // 2, width)
-    project = (qkv_weight, rate_weight)
-
-    def params(layer):
-        return (
-            first_init[layer, 0],
-            first_bias[layer],
-            second_init[layer, 0],
-            second_bias[layer].T,
-            norm_gain[layer].T,
-            norm_bias[layer].T,
-        )
-
-    mixed = run_gather(local, *project, seqs, 0)
-    o, sliced = run_scan(True, 0, 1, mixed, out_weight, *params(0))
-    middle, mixed = run_out(o, sliced, local, seqs, 2, *project)
-    o, sliced = run_scan(False, 1, 3, mixed, out_weight, *params(1))
-    (result,) = run_out(o, sliced, middle, seqs, 4)
+        name="two_layers",
+    )(local, qkv_weight, rate_weight, out_weight, *params)
     return result.reshape(tokens.shape)
 
 

time: 258 us -> 246 us (0.953)
  Pallas kernels: 252 us -> 242 us
    pallas_call x5 -> x1, Pallas kernels: 252 us -> 242 us  [body(): pl.pallas_call(functools.partial(whole_kernel, heads, shards, seqs, count...]
where the time goes in v4:
time: 246 us; the launch traced here: 244 us
  Pallas kernels  242 us (98%)
  local copies, waits for them, and re-layouts  2.95 us (1%)
    pallas_call x1, Pallas kernels, body(): pl.pallas_call(functools.partial(whole_kernel, heads, shards, seqs, count...  242 us

profile of v4, /device:TPU:8, one launch (start us, length us, event | category | flops | bytes accessed | tf_op | source)
XLA Modules:
  0.0 244.5 jit_solution(6128032168670103940)
XLA Ops:
  0.0 1.3 copy.11.refs_2_
  1.3 241.5 %two_layers.1 = bf16[2,16,3072]{2,1,0:T(8,128)(2,1)} custom-call(bf16[2,16,3072]{2,1,0:T(8,128)(2,1)} %bitcast.4, bf16[2,1,192,3072]{3,2,1,0:T(8,128)(2,1)} %refs_1_.1, bf16[2,1,3072]{2,1,0:T(2,128)(2,1)} %copy.11.refs_2_, bf16[2,64,3072]{2,1,0:T(8,128)(2,1)} %refs_3_.1, f32[2,1,64,256]{3,2,1,0:T(8,128)} %refs_4_.1, f32[2,1,256]{2,1,0:T(1,128)} %refs_5_.1, ...), custom_call_target="tpu_custom_call" | custom-call | tf_op jit(solution)/shard_map/two_layers/pallas_call | solution.py:720
  242.9 1.6 copy.13

commit v5 on v4

--- a/solution.py
+++ b/solution.py
@@ -10,6 +10,8 @@
 HEAD_SIZE = 64
 MINI = 64
 EPS = 1e-06
+EARLY = 4
+LAG = 7
 BF = jnp.bfloat16
 F32 = jnp.float32
 
@@ -96,7 +98,9 @@
     b2_ref,
     g_ref,
     c_ref,
-    o_ref,
+    early,
+    early_start,
+    early_step,
     sliced_ref,
     chain,
     outs,
@@ -240,6 +244,7 @@
                 at = spot(1 - h.x, h.z + off)
                 landed(0, at)
                 send(0, at, 3, h.twin)
+        early.go_on()
         for copy in begun:
             copy.wait_send()
 
@@ -285,6 +290,12 @@
 
     def step(j, carry):
         pl.when((j == release) & (j > 0))(send_all)
+
+        @pl.when(j == early_step)
+        def _():
+            early.begin(outs, early_start)
+
+        pl.when(j == early_step + LAG)(early.go_on)
 
         @pl.when(j < steps - 1)
         def _():
@@ -380,7 +391,6 @@
     @pl.when(active)
     def _():
         lax.fori_loop(0, steps, step, 0)
-        o_ref[...] = outs[...].reshape(o_ref.shape).astype(BF)
 
     @pl.when(jnp.logical_not(active))
     def _():
@@ -513,79 +523,110 @@
         copy.wait_send()
 
 
+class Exchange:
+    def __init__(self, heads, shards, seqs, o, blocks, joined, sem_a, sem_b, sem_c, sem_d):
+        self.heads, self.shards, self.seqs = heads, shards, seqs
+        self.o, self.blocks, self.joined = o, blocks, joined
+        self.sem_a, self.sem_b, self.sem_c, self.sem_d = sem_a, sem_b, sem_c, sem_d
+        self.copies = shards // seqs
+        self.index, self.head = lax.axis_index("seq"), lax.axis_index("head")
+        self.slot = lax.div(self.head, self.copies)
+        self.place = self.place_of(self.index)
+
+    def place_of(self, index):
+        return lax.rem(index, self.copies) * self.seqs + lax.div(index, self.copies)
+
+    def first(self, t):
+        there = lax.rem(self.head + t, self.heads)
+        return remote(
+            self.o.at[there],
+            self.blocks.at[self.slot],
+            self.sem_a.at[t],
+            self.sem_b.at[self.slot],
+            {"head": there},
+        )
+
+    def begin(self, outs, start):
+        rows = self.o.shape[1] // outs.shape[2]
+        self.o[...] = outs[:, start : start + rows].reshape(self.o.shape).astype(BF)
+        pltpu.make_async_copy(
+            self.o.at[self.head], self.blocks.at[self.slot], self.sem_b.at[self.slot]
+        ).start()
+        lax.fori_loop(1, self.heads, lambda t, c: (self.first(t).start(), c)[1], 0)
+
+    def second(self, t):
+        there = lax.rem(self.index + t, self.shards)
+        spot = self.joined.at[self.place]
+        return remote(spot, spot, self.sem_c.at[t], self.sem_d.at[self.place], {"seq": there})
+
+    def go_on(self):
+        count = self.blocks.shape[0]
+        for i in range(count):
+            pltpu.make_async_copy(self.o.at[0], self.blocks.at[i], self.sem_b.at[i]).wait()
+        self.joined[self.place] = jnp.concatenate([self.blocks[i] for i in range(count)], 1)
+        for t in range(1, self.shards):
+            self.second(t).start()
+
+    def finish(self):
+        for t in range(1, self.shards):
+            came = self.place_of(lax.rem(self.index + self.shards - t, self.shards))
+            spot = self.joined.at[came]
+            pltpu.make_async_copy(spot, spot, self.sem_d.at[came]).wait()
+
+    def settle(self, active):
+        for t in range(1, self.shards):
+            self.second(t).wait_send()
+
+        @pl.when(active)
+        def _():
+            lax.fori_loop(1, self.heads, lambda t, c: (self.first(t).wait_send(), c)[1], 0)
+
+
 def out_phase(
-    heads,
     shards,
     seqs,
-    o_ref,
+    portions,
+    starts,
+    outs,
     w_ref,
     local_ref,
     result,
-    blocks,
-    joined,
     delta,
     parts,
-    sem_a,
-    sem_b,
-    sem_c,
-    sem_d,
     sem_e,
     sem_f,
 ):
     copies = shards // seqs
     index, head = lax.axis_index("seq"), lax.axis_index("head")
-    lane = lax.rem(index, copies)
-    row = lax.div(index, copies)
-    active = lane == lax.rem(head, copies)
-    slot = lax.div(head, copies)
-
-    def first(t, to_do):
-        there = lax.rem(head + t, heads)
-        copy = remote(
-            o_ref.at[there], blocks.at[slot], sem_a.at[t], sem_b.at[slot], {"head": there}
-        )
-        to_do(copy)
-
-    keep = pltpu.make_async_copy(o_ref.at[head], blocks.at[slot], sem_b.at[slot])
+    active = lax.rem(index, copies) == lax.rem(head, copies)
+    late = portions[1]
 
     @pl.when(active)
     def _():
-        keep.start()
-        lax.fori_loop(1, heads, lambda t, c: (first(t, lambda copy: copy.start()), c)[1], 0)
-
-    size = blocks.shape[2]
-    count = blocks.shape[0]
-    for i in range(count):
-        pltpu.make_async_copy(o_ref.at[0], blocks.at[i], sem_b.at[i]).wait()
-    place = lane * seqs + row
-    joined[place] = jnp.concatenate([blocks[i] for i in range(count)], 1)
-
-    sends = []
-    for t in range(1, shards):
-        there = lax.rem(index + t, shards)
-        copy = remote(
-            joined.at[place], joined.at[place], sem_c.at[t], sem_d.at[place], {"seq": there}
-        )
-        copy.start()
-        sends.append(copy)
-    for t in range(1, shards):
-        source = lax.rem(index + shards - t, shards)
-        came = lax.rem(source, copies) * seqs + lax.div(source, copies)
-        pltpu.make_async_copy(joined.at[came], joined.at[came], sem_d.at[came]).wait()
-    rows = joined.shape[1]
-    inner = joined.shape[2]
-    total = sum(
-        jnp.dot(
-            joined[pl.ds(i * seqs, seqs)].reshape(seqs * rows, inner),
-            w_ref[i].reshape(inner, w_ref.shape[3]),
-            preferred_element_type=F32,
-        )
-        for i in range(copies)
-    )
-    delta[...] = total.reshape(delta.shape)
+        late.begin(outs, starts[1])
+
+    def product(portion, start):
+        portion.finish()
+        joined = portion.joined
+        rows, inner = joined.shape[1:]
+        total = sum(
+            jnp.dot(
+                joined[pl.ds(i * seqs, seqs)].reshape(seqs * rows, inner),
+                w_ref[i].reshape(inner, w_ref.shape[3]),
+                preferred_element_type=F32,
+            )
+            for i in range(copies)
+        )
+        count = rows // delta.shape[2]
+        delta[:, start : start + count] = total.reshape(seqs, count, *delta.shape[2:])
+
+    product(portions[0], starts[0])
+    late.go_on()
+    product(late, starts[1])
 
     mine = pltpu.make_async_copy(delta.at[:, index], parts.at[index], sem_f.at[index])
     mine.start()
+    sends = []
     for t in range(1, shards):
         there = lax.rem(index + t, shards)
         copy = remote(
@@ -596,7 +637,6 @@
     for i in range(shards):
         pltpu.make_async_copy(delta.at[:, 0], parts.at[i], sem_f.at[i]).wait()
     cut = parts.shape[3]
-    tokens = result.shape[0] * result.shape[1]
     for i in range(shards):
         columns = slice(i * cut, (i + 1) * cut)
         summed = local_ref[:, :, columns].astype(F32) + parts[i].reshape(
@@ -605,10 +645,8 @@
         result[:, :, columns] = summed.astype(BF)
     for copy in sends:
         copy.wait_send()
-
-    @pl.when(active)
-    def _():
-        lax.fori_loop(1, heads, lambda t, c: (first(t, lambda copy: copy.wait_send()), c)[1], 0)
+    for portion in portions:
+        portion.settle(active)
 
 
 def whole_kernel(heads, shards, seqs, counts, *refs):
@@ -633,8 +671,10 @@
     greet(others("head", heads) + others("seq", shards))
     for layer in range(2):
         mixed, *gather = take(counts[1])
-        sliced, o, *scan = take(counts[2])
-        out = take(counts[3])
+        sliced, *scan = take(counts[2])
+        portions = [Exchange(heads, shards, seqs, *take(counts[3])) for _ in range(2)]
+        out = take(counts[4])
+        starts = (0, EARLY) if layer == 0 else (shards - EARLY, 0)
         source, target = (local, middle) if layer == 0 else (middle, result)
         full, *sems = gather
         gather_project(layer, source, qkv_ref, rate_ref, mixed, full, weight, *sems)
@@ -650,14 +690,16 @@
             mixed,
             weight_ref,
             *held,
-            o,
+            portions[0],
+            starts[0],
+            EARLY * (heads * local.shape[0] * local.shape[1] // seqs // MINI) + 1,
             sliced,
             chain,
             outs,
             *scan_sems,
             *state,
         )
-        out_phase(heads, shards, seqs, o, sliced, source, target, *out)
+        out_phase(shards, seqs, portions, starts, outs, sliced, source, target, *out)
 
 
 def body(tokens, qkv_weight, rate_weight, *rest):
@@ -695,28 +737,31 @@
     ]
     scan = [
         pltpu.VMEM((copies, count, size, cut), BF),
-        pltpu.VMEM((heads, shards * rows, size), BF),
         pltpu.VMEM((shards * heads, rows, 4 * size), F32),
         dma((seqs, minis)),
         dma((shards * minis,)),
         dma((4, 2, count)),
         dma((2, count)),
     ]
-    out = [
-        pltpu.VMEM((count, shards * rows, size), BF),
-        pltpu.VMEM((shards, shards * rows, count * size), BF),
-        pltpu.VMEM((seqs, shards, rows, cut), F32),
-        pltpu.VMEM((shards, seqs, rows, cut), F32),
+    portion = lambda many: [
+        pltpu.VMEM((heads, many * rows, size), BF),
+        pltpu.VMEM((count, many * rows, size), BF),
+        pltpu.VMEM((shards, many * rows, count * size), BF),
         dma((heads,)),
         dma((count,)),
         dma((shards,)),
         dma((shards,)),
+    ]
+    out = [
+        pltpu.VMEM((seqs, shards, rows, cut), F32),
+        pltpu.VMEM((shards, seqs, rows, cut), F32),
         dma((shards,)),
         dma((shards,)),
     ]
+    layer = gather + scan + portion(EARLY) + portion(shards - EARLY) + out
     hbm = pl.BlockSpec(memory_space=pltpu.HBM)
     vmem = pl.BlockSpec(memory_space=pltpu.VMEM)
-    counts = (len(state), len(gather), len(scan), len(out))
+    counts = (len(state), len(gather), len(scan), len(portion(1)), len(out))
     result = pl.pallas_call(
         functools.partial(whole_kernel, heads, shards, seqs, counts),
         out_shape=jax.ShapeDtypeStruct(local.shape, BF),
@@ -729,8 +774,8 @@
             dma((len(params),)),
             *[pltpu.VMEM(param.shape, F32) for param in params],
             *state,
-            *(gather + scan + out),
-            *(gather + scan + out),
+            *layer,
+            *layer,
         ],
         compiler_params=pltpu.CompilerParams(
             vmem_limit_bytes=63 * 2**20, collective_id=0, has_side_effects=True

time: 246 us -> 229 us (0.931)
  Pallas kernels: 242 us -> 225 us
    pallas_call x1, Pallas kernels: 242 us -> 225 us  [body(): pl.pallas_call(functools.partial(whole_kernel, heads, shards, seqs, count...]
where the time goes in v5:
time: 229 us; the launch traced here: 228 us
  Pallas kernels  225 us (98%)
  local copies, waits for them, and re-layouts  2.95 us (1%)
    pallas_call x1, Pallas kernels, body(): pl.pallas_call(functools.partial(whole_kernel, heads, shards, seqs, count...  225 us

profile of v5, /device:TPU:8, one launch (start us, length us, event | category | flops | bytes accessed | tf_op | source)
XLA Modules:
  0.0 228.1 jit_solution(5418174763992473885)
XLA Ops:
  0.0 1.3 copy.11.refs_2_
  1.3 225.1 %two_layers.1 = bf16[2,16,3072]{2,1,0:T(8,128)(2,1)} custom-call(bf16[2,16,3072]{2,1,0:T(8,128)(2,1)} %bitcast.4, bf16[2,1,192,3072]{3,2,1,0:T(8,128)(2,1)} %refs_1_.1, bf16[2,1,3072]{2,1,0:T(2,128)(2,1)} %copy.11.refs_2_, bf16[2,64,3072]{2,1,0:T(8,128)(2,1)} %refs_3_.1, f32[2,1,64,256]{3,2,1,0:T(8,128)} %refs_4_.1, f32[2,1,256]{2,1,0:T(1,128)} %refs_5_.1, ...), custom_call_target="tpu_custom_call" | custom-call | tf_op jit(solution)/shard_map/two_layers/pallas_call | solution.py:765
  226.5 1.6 copy.13

commit v6 on v5

--- a/solution.py
+++ b/solution.py
@@ -516,8 +516,8 @@
             hand_over(k - 1)
         if k > 2:
             project_at(k - 2)
+    project_at(last - 1)
     hand_over(last)
-    project_at(last - 1)
     project_at(last)
     for copy in started:
         copy.wait_send()

time: 229 us -> 231 us (level)
  Pallas kernels: 225 us -> 228 us
    pallas_call x1, Pallas kernels: 225 us -> 228 us  [body(): pl.pallas_call(functools.partial(whole_kernel, heads, shards, seqs, count...]
where the time goes in v6:
time: 231 us
  Pallas kernels  228 us (99%)
  local copies, waits for them, and re-layouts  2.95 us (1%)
    pallas_call x1, Pallas kernels, body(): pl.pallas_call(functools.partial(whole_kernel, heads, shards, seqs, count...  228 us

profile of v6, /device:TPU:8, one launch (start us, length us, event | category | flops | bytes accessed | tf_op | source)
XLA Modules:
  0.0 230.5 jit_solution(11355566772052698095)
XLA Ops:
  0.0 1.3 copy.11.refs_2_
  1.3 227.5 %two_layers.1 = bf16[2,16,3072]{2,1,0:T(8,128)(2,1)} custom-call(bf16[2,16,3072]{2,1,0:T(8,128)(2,1)} %bitcast.4, bf16[2,1,192,3072]{3,2,1,0:T(8,128)(2,1)} %refs_1_.1, bf16[2,1,3072]{2,1,0:T(2,128)(2,1)} %copy.11.refs_2_, bf16[2,64,3072]{2,1,0:T(8,128)(2,1)} %refs_3_.1, f32[2,1,64,256]{3,2,1,0:T(8,128)} %refs_4_.1, f32[2,1,256]{2,1,0:T(1,128)} %refs_5_.1, ...), custom_call_target="tpu_custom_call" | custom-call | tf_op jit(solution)/shard_map/two_layers/pallas_call | solution.py:765
  228.9 1.6 copy.13
